TPU v7x, 512 devices: a whole 4x8x8 slice. The times are simulated.
512 devices in a mesh: hst: 8 (over z), dev: 64 (over x, y, core).
Axes of the slice: x: 4, y: 8, z: 8, core: 2. Of those that a mesh axis runs over, the one named last changes fastest.
Arguments:
- feats: bfloat16 [131072, 256], P(('hst', 'dev')), may hold values from -6 to 6
- grad_out: bfloat16 [131072, 256], P(('hst', 'dev')), may hold values from -6 to 6
- preact: bfloat16 [131072, 256], P(('hst', 'dev')), may hold values from -6 to 6
- neigh_agg: bfloat16 [131072, 256], P(('hst', 'dev')), may hold values from -6 to 6
- cross_coords: bfloat16 [131072, 64], P(('hst', 'dev')), may hold values from -6 to 6
- w_self: bfloat16 [256, 256], replicated, may hold values from -0.375 to 0.375
- w_neigh: bfloat16 [256, 256], replicated, may hold values from -0.375 to 0.375
- proj: bfloat16 [256, 64], replicated, may hold values from -0.375 to 0.375
- lift: bfloat16 [64, 256], replicated, may hold values from -0.75 to 0.75
- tile_values: bfloat16 [16384, 128, 128], P(('hst', 'dev')), may hold values from -0.21875 to 0.21875
- tile_rows: int32 [512, 32], P(('hst', 'dev')), may hold values from 0 to 1
- tile_cols: int32 [512, 32], P(('hst', 'dev')), may hold values from 0 to 5
- tile_ids: int32 [512, 32], P(('hst', 'dev')), may hold values from 0 to 31
- cross_rows: int32 [512, 8], P(('hst', 'dev')), may hold values from 0 to 1
- cross_cols: int32 [512, 8], P(('hst', 'dev')), may hold values from 0 to 7
- cross_ids: int32 [512, 8], P(('hst', 'dev')), may hold values from 0 to 31
- send_counts: int32 [512, 64], P(('hst', 'dev')), may hold values from 1 to 8, as said below
- recv_rows: int32 [512, 64, 8], P(('hst', 'dev')), may hold values from 0 to 255
- cross_counts: int32 [512, 8], P(('hst', 'dev')), may hold values from 1 to 128, as said below
- cross_recv_rows: int32 [512, 8, 128], P(('hst', 'dev')), may hold values from 0 to 255
Outputs:
- grad_feats: bfloat16 [131072, 256], P(('hst', 'dev'))
- grad_self: float32 [256, 256], replicated
- grad_neigh: float32 [256, 256], replicated
- grad_lift: float32 [64, 256], replicated
- grad_proj: float32 [256, 64], replicated
Inputs may be any that keep to these rules, and one draw needn't show every extreme that they name: `send_counts`: slot k toward peer q is live when k < the count; each partition fills all 8 slots toward the next peer of its group. `cross_counts`: slot k toward group g is live when k < the count; each partition fills all 128 slots toward the next group.
All inputs are finite; a program needn't handle non-finite values.
Results may differ from a plain program's by a relative error of at most 0.0058.
Values may be sent and summed in bfloat16 or wider, within the bound.
No kernel may reach another device: no remote copies, remote signals or barrier semaphores. Data moves between devices by JAX's collectives and lax.ppermute only.
A program may use at most 64 MiB of HBM per device.

v0:
```python
import math

import jax
import jax.numpy as jnp
from jax import lax
from jax.sharding import PartitionSpec as P


def sweep(tile_vals, row_blocks, col_blocks, tile_index, grads, blocks, per_group):
    features = grads.shape[1]
    pieces = grads.reshape(-1, 128, features)
    groups = row_blocks.shape[0] // per_group

    def advance(running, listed):
        row_part, col_part, index_part = listed
        product = jnp.einsum(
            "tij,tif->tjf",
            tile_vals[index_part],
            pieces[row_part],
            preferred_element_type=jnp.float32,
        )
        return (running.at[col_part].add(product), None)

    initial = jnp.zeros((blocks, 128, features), jnp.float32)
    listing = (
        row_blocks.reshape(groups, per_group),
        col_blocks.reshape(groups, per_group),
        tile_index.reshape(groups, per_group),
    )
    running, unused = lax.scan(advance, initial, listing)
    return running.reshape(blocks * 128, features)


def body(
    feats,
    grad_out,
    preact,
    neigh_agg,
    cross_coords,
    w_self,
    w_neigh,
    proj,
    lift,
    tile_values,
    tile_rows,
    tile_cols,
    tile_ids,
    cross_rows,
    cross_cols,
    cross_ids,
    send_counts,
    recv_rows,
    cross_counts,
    cross_recv_rows,
):
    node_rows = feats.shape[0]
    features = feats.shape[1]
    rank_width = proj.shape[1]
    peers = lax.axis_size("dev")
    groups = lax.axis_size("hst")
    slot_cap = recv_rows.shape[-1]
    cross_cap = cross_recv_rows.shape[-1]
    own_blocks = node_rows // 128
    tiles_per_block = tile_rows.shape[-1] // own_blocks
    cross_per_block = cross_rows.shape[-1] // own_blocks
    norm_scale = 1.0 / math.sqrt(node_rows * peers * groups)
    grad_pre = jnp.where(preact > 0, grad_out.astype(jnp.float32), 0.0).astype(jnp.bfloat16)
    grad_self = norm_scale * jnp.dot(feats.T, grad_pre, preferred_element_type=jnp.float32)
    grad_neigh = norm_scale * jnp.dot(neigh_agg.T, grad_pre, preferred_element_type=jnp.float32)
    grad_lift = norm_scale * jnp.dot(cross_coords.T, grad_pre, preferred_element_type=jnp.float32)
    neigh_grad = jnp.dot(grad_pre, w_neigh.T, preferred_element_type=jnp.float32).astype(
        jnp.bfloat16
    )
    coord_grad = jnp.dot(grad_pre, lift.T, preferred_element_type=jnp.float32).astype(jnp.bfloat16)
    col_total = own_blocks + peers * slot_cap // 128
    inner_sum = sweep(
        tile_values,
        tile_rows.reshape(-1),
        tile_cols.reshape(-1),
        tile_ids.reshape(-1),
        neigh_grad,
        col_total,
        tiles_per_block,
    )
    slot_index = jnp.arange(slot_cap)
    boundary = inner_sum[node_rows:].reshape(peers, slot_cap, features)
    live_mask = slot_index[None, :] < send_counts.reshape(-1)[:, None]
    boundary = jnp.where(live_mask[:, :, None], boundary, 0.0).astype(jnp.bfloat16)
    arrived = lax.all_to_all(boundary, "dev", split_axis=0, concat_axis=0, tiled=True)
    cross_sum = sweep(
        tile_values,
        cross_rows.reshape(-1),
        cross_cols.reshape(-1),
        cross_ids.reshape(-1),
        coord_grad,
        groups * cross_cap // 128,
        cross_per_block,
    )
    cross_sum = cross_sum.reshape(groups, cross_cap, rank_width)
    cross_slot = jnp.arange(cross_cap)
    cross_mask = cross_slot[None, :] < cross_counts.reshape(-1)[:, None]
    cross_part = jnp.where(cross_mask[:, :, None], cross_sum, 0.0).astype(jnp.bfloat16)
    coords_in = lax.all_to_all(cross_part, "hst", split_axis=0, concat_axis=0, tiled=True)
    landed = (
        jnp.zeros((node_rows, features), jnp.float32)
        .at[recv_rows.reshape(-1)]
        .add(arrived.reshape(-1, features).astype(jnp.float32))
    )
    coords = (
        jnp.zeros((node_rows, rank_width), jnp.float32)
        .at[cross_recv_rows.reshape(-1)]
        .add(coords_in.reshape(-1, rank_width).astype(jnp.float32))
    )
    coords = coords.astype(jnp.bfloat16)
    grad_proj = norm_scale * jnp.dot(feats.T, coords, preferred_element_type=jnp.float32)
    grad_feats = jnp.dot(grad_pre, w_self.T, preferred_element_type=jnp.float32)
    grad_feats = grad_feats + inner_sum[:node_rows] + landed
    grad_feats = grad_feats + jnp.dot(coords, proj.T, preferred_element_type=jnp.float32)
    grad_self, grad_neigh, grad_lift, grad_proj = lax.psum(
        (grad_self, grad_neigh, grad_lift, grad_proj), ("hst", "dev")
    )
    return (grad_feats.astype(jnp.bfloat16), grad_self, grad_neigh, grad_lift, grad_proj)


def solution(mesh):
    placed = (
        P(("hst", "dev"), None),
        P(("hst", "dev"), None),
        P(("hst", "dev"), None),
        P(("hst", "dev"), None),
        P(("hst", "dev"), None),
        P(),
        P(),
        P(),
        P(),
        P(("hst", "dev"), None, None),
        P(("hst", "dev"), None),
        P(("hst", "dev"), None),
        P(("hst", "dev"), None),
        P(("hst", "dev"), None),
        P(("hst", "dev"), None),
        P(("hst", "dev"), None),
        P(("hst", "dev"), None),
        P(("hst", "dev"), None, None),
        P(("hst", "dev"), None),
        P(("hst", "dev"), None, None),
    )
    return jax.shard_map(
        body,
        mesh=mesh,
        in_specs=placed,
        out_specs=(P(("hst", "dev"), None), P(), P(), P(), P()),
        check_vma=False,
    )
```

profile of v0, /device:TPU:1, one launch (start us, length us, event | category | flops | bytes accessed | tf_op | source)
XLA Modules:
  0.0 363.4 jit_solution(3683046797034559694)
XLA Ops:
  7.2 1.0 select_convert_fusion.2
  8.2 0.9 convolution_convert_fusion.1
  9.3 0.5 broadcast.221
  9.8 1.3 reduce.18
  11.2 1.3 reduce.19
  12.6 1.3 reduce.20
  14.1 6.8 %while.21 = (s32[]{:T(128)}, f32[8,128,64]{1,2,0:T(8,128)S(1)}, s32[2,4]{1,0:T(2,128)S(1)}, s32[2,4]{1,0:T(2,128)S(1)}, bf16[32,128,128]{2,1,0:T(8,128)(2,1)}, /...) while((s32[]{:T(128)}, f32[8,128,64]{1,2,0:T(8,128)S(1)}, s32[2,4]{1,0:T(2,128)S(1)}, ...), condition=%wide.region_5.6_spmd, body=%wide.region_3.5_spmd.sunk | while | flops 8423462 | bytes 1122573 | solution.py:30
  14.1 1.8 gather_fusion.2
  16.0 0.6 gather_fusion.3
  16.8 0.7 scatter_fusion.1
  17.5 1.8 gather_fusion.2
  19.4 0.6 gather_fusion.3
  20.2 0.7 scatter_fusion.1
  21.0 0.7 select_convert_fusion.1
  21.7 10.9 %all-to-all-start = ((bf16[8,128,64]{1,2,0:T(8,128)(2,1)}), bf16[8,128,64]{1,2,0:T(8,128)(2,1)S(1)}, u32[]{:S(2)}, u32[]{:S(2)}) async-start(bf16[8,128,64]{1,2,0:T(8,128)(2,1)} %select_convert_fusion.1), calls=%async_computation | async-start | bytes 262144 | tf_op jit(solution)/shard_map/all_to_all | solution.py:103
  32.8 0.7 reduce.21
  33.5 0.7 reduce.22
  34.3 0.7 reduce.23
  34.9 0.6 reshape_reshape.20
  35.7 18.2 %while.20 = (s32[]{:T(128)}, f32[6,128,256]{2,1,0:T(8,128)S(1)}, s32[2,16]{1,0:T(2,128)S(1)}, s32[2,16]{1,0:T(2,128)S(1)}, bf16[32,128,128]{2,1,0:T(8,128)(2,1)}...) while((s32[]{:T(128)}, f32[6,128,256]{2,1,0:T(8,128)S(1)}, s32[2,16]{1,0:T(2,128)S(1)}, ...), condition=%wide.region_2.3_spmd, body=%wide.region_0.2_spmd.sunk | while | flops 134744208 | bytes 13116189 | solution.py:30
  35.7 2.7 gather_fusion
  38.4 0.7 fusion.58
  39.1 1.6 gather_fusion.1
  40.7 1.9 fusion.59
  42.6 2.2 scatter_fusion
  44.8 2.7 gather_fusion
  47.5 0.7 fusion.58
  48.2 1.6 gather_fusion.1
  49.8 1.9 fusion.59
  51.7 2.2 scatter_fusion
  53.9 0.7 compare_select_fusion.6
  54.6 0.7 iota_compare_fusion
  55.6 0.9 fusion.12
  56.5 0.9 fusion.13
  57.4 0.8 select_convert_fusion
  58.3 0.8 fusion.15
  59.1 11.1 %all-to-all-start.1 = ((bf16[64,8,256]{2,1,0:T(8,128)(2,1)}), bf16[64,8,256]{2,1,0:T(8,128)(2,1)S(1)}, u32[]{:S(2)}, u32[]{:S(2)}) async-start(bf16[64,8,256]{2,1,0:T(8,128)(2,1)} %select_convert_fusion), calls=%async_computation.1 | async-start | bytes 524288 | tf_op jit(solution)/shard_map/all_to_all | solution.py:89
  70.4 6.1 %scatter_custom_fusion.2 = f32[256,64]{1,0:T(8,128)S(1)} fusion(s32[1024]{0:T(1024)S(1)} %bitcast.120, f32[1024,64]{1,0:T(8,128)S(1)} %bitcast.118, f32[]{:T(128)} %constant.30.clone.1), kind=kCustom, calls=%fused_computation.54 | custom fusion | flops 65536 | bytes 65540 | tf_op jit(solution)/shard_map/scatter-add | solution.py:112
  76.4 0.8 fusion.16
  77.5 0.2 fusion.14
  77.7 4.5 %all-to-all-done.1 = bf16[64,8,256]{2,1,0:T(8,128)(2,1)S(1)} async-done(((bf16[64,8,256]{2,1,0:T(8,128)(2,1)}), bf16[64,8,256]{2,1,0:T(8,128)(2,1)S(1)}, u32[]{:S(2)}, u32[]{:S(2)}) %all-to-all-start.1) | async-done | bytes 262176 | tf_op jit(solution)/shard_map/all_to_all | solution.py:89
  82.2 3.5 scatter_custom_fusion.3
  85.6 0.7 convert_element_type.47
  86.3 263.7 %all-reduce.3.cloned.1.call-done = (f32[256,256]{0,1:T(8,128)}, f32[256,256]{0,1:T(8,128)}, f32[64,256]{1,0:T(8,128)}, f32[256,64]{0,1:T(8,128)}) async-done(((f32[256,256]{0,1:T(8,128)}, f32[256,256]{0,1:T(8,128)}, f32[64,256]{1,0:T(8,128)}, f32[256,64]{0,1:T(8,128)}), (f32[256,256]{0,1:T(8,128)}, f32[256,256]{0,1:T(8,128)}, f32[64,256]{1,0:T(8,128)}, f32[256,64]{0,1:T(8,128)})) %all-reduce.3.cloned.1.call-update) | async-done | bytes 655376 | tf_op jit(solution)/shard_map/psum | solution.py:119
  350.0 1.8 copy.43
  351.8 1.8 copy.44
  353.6 1.5 copy.70
  355.0 1.5 copy.71
  (58 shorter events, 2.1 us)
Async XLA Ops:
  7.2 49.3 %copy-start = (bf16[256,256]{1,0:T(8,128)(2,1)S(1)}, bf16[256,256]{1,0:T(8,128)(2,1)}, u32[]{:S(2)}) copy-start(bf16[256,256]{1,0:T(8,128)(2,1)} %param.24) | copy-start | bytes 393220
  14.0 6.8 %copy-start.7 = (s32[1,8]{1,0:T(1,128)S(1)}, s32[1,8]{1,0:T(1,128)}, u32[]{:S(2)}) copy-start(s32[1,8]{1,0:T(1,128)} %param.42) | copy-start | bytes 100
  14.1 18.5 %copy-start.1 = (bf16[256,256]{1,0:T(8,128)(2,1)S(1)}, bf16[256,256]{1,0:T(8,128)(2,1)}, u32[]{:S(2)}) copy-start(bf16[256,256]{1,0:T(8,128)(2,1)} %param.30) | copy-start | bytes 393220
  14.1 18.7 %copy-start.8 = (s32[1,32]{1,0:T(1,128)S(1)}, s32[1,32]{1,0:T(1,128)}, u32[]{:S(2)}) copy-start(s32[1,32]{1,0:T(1,128)} %param.35) | copy-start | bytes 388
  14.1 19.4 %copy-start.9 = (s32[1,32]{1,0:T(1,128)S(1)}, s32[1,32]{1,0:T(1,128)}, u32[]{:S(2)}) copy-start(s32[1,32]{1,0:T(1,128)} %param.36) | copy-start | bytes 388
  14.1 20.2 %copy-start.10 = (s32[1,32]{1,0:T(1,128)S(1)}, s32[1,32]{1,0:T(1,128)}, u32[]{:S(2)}) copy-start(s32[1,32]{1,0:T(1,128)} %param.34) | copy-start | bytes 388
  21.7 37.4 %all-to-all-start = ((bf16[8,128,64]{1,2,0:T(8,128)(2,1)}), bf16[8,128,64]{1,2,0:T(8,128)(2,1)S(1)}, u32[]{:S(2)}, u32[]{:S(2)}) async-start(bf16[8,128,64]{1,2,0:T(8,128)(2,1)} %select_convert_fusion.1), calls=%async_computation | async-start | bytes 262144 | tf_op jit(solution)/shard_map/all_to_all | solution.py:103
  35.7 19.7 %copy-start.6 = (s32[1,64,8]{1,2,0:T(8,128)S(1)}, s32[1,64,8]{1,2,0:T(8,128)}, u32[]{:S(2)}) copy-start(s32[1,64,8]{1,2,0:T(8,128)} %param.41) | copy-start | bytes 6148
  35.7 19.9 %copy-start.2 = (bf16[256,256]{1,0:T(8,128)(2,1)S(1)}, bf16[256,256]{1,0:T(8,128)(2,1)}, u32[]{:S(2)}) copy-start(bf16[256,256]{1,0:T(8,128)(2,1)} %param.27) | copy-start | bytes 393220
  53.9 4.4 %copy-start.4 = (bf16[256,64]{0,1:T(8,128)(2,1)S(1)}, bf16[256,64]{0,1:T(8,128)(2,1)}, u32[]{:S(2)}) copy-start(bf16[256,64]{0,1:T(8,128)(2,1)} %param.28) | copy-start | bytes 98308
  55.4 21.9 %copy-start.5 = (bf16[256,64]{0,1:T(8,128)(2,1)S(1)}, bf16[256,64]{0,1:T(8,128)(2,1)}, u32[]{:S(2)}) copy-start(bf16[256,64]{0,1:T(8,128)(2,1)} %param.31) | copy-start | bytes 98308
  56.5 20.9 %copy-start.3 = (bf16[256,256]{1,0:T(8,128)(2,1)S(1)}, bf16[256,256]{1,0:T(8,128)(2,1)}, u32[]{:S(2)}) copy-start(bf16[256,256]{1,0:T(8,128)(2,1)} %param.29) | copy-start | bytes 393220
  59.1 23.1 %all-to-all-start.1 = ((bf16[64,8,256]{2,1,0:T(8,128)(2,1)}), bf16[64,8,256]{2,1,0:T(8,128)(2,1)S(1)}, u32[]{:S(2)}, u32[]{:S(2)}) async-start(bf16[64,8,256]{2,1,0:T(8,128)(2,1)} %select_convert_fusion), calls=%async_computation.1 | async-start | bytes 524288 | tf_op jit(solution)/shard_map/all_to_all | solution.py:89
  70.2 279.8 %all-reduce.3.cloned.1.call-start = ((), (), s32[]{:S(2)}) async-start(), calls=%async_computation.2 | async-start | bytes 1310720 | tf_op jit(solution)/shard_map/psum | solution.py:119
Sparse Core Ops, SparseCore 0:
  77.4 272.5 all-reduce.2
where the time goes:
time: 365 us; the launch traced here: 363 us
  waiting for transfers between devices  268 us (73%)
  other arithmetic  27.5 us (8%)
  local copies, waits for them, and re-layouts  22.1 us (6%)
  starting transfers between devices  22 us (6%)
  between operations  14.3 us (4%)
  matrix products  9.11 us (2%)
    psum x1, waiting for transfers between devices, body(): lax.psum((grad_self, grad_neigh, grad_lift, grad_proj), ('hst', 'dev'))  264 us
    all_to_all x1, starting transfers between devices, body(): lax.all_to_all(boundary, 'dev', split_axis=0, concat_axis=0, tiled=True)  11.1 us
    all_to_all x1, starting transfers between devices, body(): lax.all_to_all(cross_part, 'hst', split_axis=0, concat_axis=0, tiled=True)  10.9 us
    gather x4, local copies, waits for them, and re-layouts, advance(): tile_vals[index_part]  8.96 us
  transfers between devices with their start and end apart: 3, of which 2 were waited for; matrix products, arithmetic and copies ran while one was open for 10% of the time, Pallas kernels for 0%

commit v1 on v0

v1 whole, which is shorter than its diff:
```python
import math

import jax
import jax.numpy as jnp
from jax import lax
from jax.experimental import pallas as pl
from jax.experimental.pallas import tpu as pltpu
from jax.sharding import PartitionSpec as P

F32 = jnp.float32
BF16 = jnp.bfloat16
BLOCK = 128

VMEM = pl.BlockSpec(memory_space=pltpu.VMEM)
SMEM = pl.BlockSpec(memory_space=pltpu.SMEM)


def dot_nn(a, b):
    return jnp.dot(a, b, preferred_element_type=F32)


def dot_nt(a, b):
    return lax.dot_general(a, b, (((1,), (1,)), ((), ())), preferred_element_type=F32)


def dot_tn(a, b):
    return lax.dot_general(a, b, (((0,), (0,)), ((), ())), preferred_element_type=F32)


def call(kernel, outs, specs, args, scratch=(), flops=0):
    nbytes = sum(math.prod(o.shape) * o.dtype.itemsize for o in list(outs) + list(args))
    return pl.pallas_call(
        kernel,
        out_shape=tuple(outs),
        in_specs=specs,
        out_specs=tuple(VMEM for _ in outs),
        scratch_shapes=list(scratch),
        compiler_params=pltpu.CompilerParams(vmem_limit_bytes=40 * 1024 * 1024),
        cost_estimate=pl.CostEstimate(flops=flops, bytes_accessed=nbytes, transcendentals=0),
    )(*args)


def shape(dims, dtype):
    return jax.ShapeDtypeStruct(dims, dtype)


def first_kernel(
    xrow, xcol, xid, xcount, grad_out, preact, feats, neigh_agg, cross_coords, lift, tiles,
    gp_out, s1_out, lift_out, cg, acc,
):
    groups = acc.shape[0]
    rank = acc.shape[1]
    gp = jnp.where(preact[...].astype(F32) > 0, grad_out[...].astype(F32), 0.0).astype(BF16)
    gp_out[...] = gp
    cgt = dot_nt(lift[...], gp).astype(BF16)
    for b in range(cg.shape[0]):
        cg[b] = cgt[:, b * BLOCK : (b + 1) * BLOCK]
    acc[...] = jnp.zeros_like(acc)
    for t in range(xrow.shape[1]):
        col = xcol[0, t]
        acc[col] += dot_nn(cg[xrow[0, t]], tiles[xid[0, t]])
    slot = lax.broadcasted_iota(jnp.int32, (rank, BLOCK), 1)
    for j in range(groups):
        s1_out[j, 0:rank, :] = jnp.where(slot < xcount[0, j], acc[j], 0.0).astype(BF16)
    at = rank
    for source in (feats, neigh_agg):
        part = dot_tn(source[...], gp).astype(BF16)
        step = part.shape[0] // groups
        for j in range(groups):
            rows = part[j * step : (j + 1) * step]
            s1_out[j, at : at + step, :] = rows[:, :BLOCK]
            s1_out[j, at + step : at + 2 * step, :] = rows[:, BLOCK:]
        at += 2 * step
    lift_out[...] = dot_tn(cross_coords[...], gp)


def inner_kernel(trow, tcol, tid, counts, gp, w_neigh, w_self, tiles, base_out, bnd_out, ng, acc):
    cap = bnd_out.shape[1]
    blocks = ng.shape[0]
    own = dot_nt(gp[...], w_self[...])
    grad = dot_nt(gp[...], w_neigh[...]).astype(BF16)
    for b in range(blocks):
        ng[b] = grad[b * BLOCK : (b + 1) * BLOCK]
    acc[...] = jnp.zeros_like(acc)
    for t in range(trow.shape[1]):
        col = tcol[0, t]
        acc[col] += dot_tn(tiles[tid[0, t]], ng[trow[0, t]])
    for b in range(blocks):
        base_out[b * BLOCK : (b + 1) * BLOCK, :] = own[b * BLOCK : (b + 1) * BLOCK] + acc[b]
    slot = lax.broadcasted_iota(jnp.int32, (cap, acc.shape[2]), 0)
    per_block = BLOCK // cap
    for q in range(bnd_out.shape[0]):
        rows = acc[blocks + q // per_block, (q % per_block) * cap : (q % per_block + 1) * cap, :]
        bnd_out[q] = jnp.where(slot < counts[0, q], rows, 0.0)


def split_rows(value):
    high = value.astype(BF16).astype(F32)
    return high, value - high


def second_kernel(s1, xrecv, feats, lift_part, bnd, coords_out, s2_out, scr):
    groups = s1.shape[0]
    rank = lift_part.shape[0]
    peers = bnd.shape[0]
    cap = bnd.shape[1]
    nodes = feats.shape[0]
    row = lax.broadcasted_iota(jnp.int32, (nodes, BLOCK), 0)
    total = None
    for g in range(groups):
        hot = jnp.where(row == xrecv[g : g + 1, :], 1.0, 0.0).astype(BF16)
        term = dot_nt(s1[g, 0:rank, :], hot)
        total = term if total is None else total + term
    coords_t = total.astype(BF16)
    coords_out[...] = total.T.astype(BF16)
    proj_t = dot_nn(coords_t, feats[...])
    summed = s1[0, rank:, :].astype(F32)
    for g in range(1, groups):
        summed = summed + s1[g, rank:, :].astype(F32)
    scr[...] = jnp.zeros_like(scr)
    wide = 2 * cap
    for q in range(peers):
        scr[0, q * wide : q * wide + cap, :] = bnd[q, :, :BLOCK]
        scr[1, q * wide : q * wide + cap, :] = bnd[q, :, BLOCK:]
    for half in range(2):
        lanes = slice(half * BLOCK, (half + 1) * BLOCK)
        pieces = (
            summed[half * peers : (half + 1) * peers],
            proj_t[:, lanes],
            lift_part[:, lanes],
        )
        for at, piece in enumerate(pieces):
            high, low = split_rows(piece)
            scr[half, pl.ds(cap + at, peers, stride=wide), :] = high
            scr[half, pl.ds(cap + 3 + at, peers, stride=wide), :] = low
        s2_out[:, lanes] = scr[half].astype(BF16)


def third_kernel(s2, s3_out):
    count = s2.shape[0]
    wide = 16
    kind = lax.rem(lax.broadcasted_iota(jnp.int32, (16, count), 1), wide) - wide // 2
    want = lax.broadcasted_iota(jnp.int32, (16, count), 0)
    pick = (want < 3) & ((kind == want) | (kind == want + 3))
    sums = dot_nn(jnp.where(pick, 1.0, 0.0).astype(BF16), s2[...])
    flat = jnp.concatenate(
        [sums[i : i + 1, h * BLOCK : (h + 1) * BLOCK] for i in range(3) for h in range(2)]
        + [jnp.zeros((2, BLOCK), F32)],
        axis=0,
    )
    for j in range(s3_out.shape[0]):
        s3_out[j] = flat


def feats_kernel(s2, recv, base, coords, proj, out):
    nodes = base.shape[0]
    row = lax.broadcasted_iota(jnp.int32, (nodes, recv.shape[1]), 0)
    hot = jnp.where(row == recv[...], 1.0, 0.0).astype(BF16)
    value = base[...] + dot_nn(hot, s2[...]) + dot_nt(coords[...], proj[...])
    out[...] = value.astype(BF16)


def fourth_kernel(s3, s4_out):
    groups = s3.shape[0]
    total = s3[0]
    for g in range(1, groups):
        total = total + s3[g]
    share = jnp.concatenate(
        [s3[g, 0:1, :] for g in range(groups)]
        + [s3[g, 1:2, :] for g in range(groups)]
        + [total[2:6], jnp.zeros((4, BLOCK), F32)],
        axis=0,
    ).astype(BF16)
    for j in range(s4_out.shape[0]):
        s4_out[j] = share


def last_kernel(norm_scale, s4, self_out, neigh_out, lift_out, proj_out, scr):
    peers, rows = s4.shape[0], s4.shape[1]
    half = peers // 2
    for j in range(peers):
        scr[j * rows : (j + 1) * rows, :] = s4[j].astype(F32) * norm_scale
    for at, out in ((0, self_out), (8, neigh_out)):
        for g in range(8):
            for h in range(2):
                out[g * half : (g + 1) * half, h * BLOCK : (h + 1) * BLOCK] = scr[
                    pl.ds(h * half * rows + at + g, half, stride=rows), :
                ]
    for h in range(2):
        piece = scr[pl.ds(16 + h, peers, stride=rows), :]
        proj_out[h * BLOCK : (h + 1) * BLOCK, :] = piece.T
        lift_out[:, h * BLOCK : (h + 1) * BLOCK] = scr[pl.ds(18 + h, peers, stride=rows), :]


def body(
    feats,
    grad_out,
    preact,
    neigh_agg,
    cross_coords,
    w_self,
    w_neigh,
    proj,
    lift,
    tile_values,
    tile_rows,
    tile_cols,
    tile_ids,
    cross_rows,
    cross_cols,
    cross_ids,
    send_counts,
    recv_rows,
    cross_counts,
    cross_recv_rows,
):
    nodes, width = feats.shape
    rank = proj.shape[1]
    peers = lax.axis_size("dev")
    groups = lax.axis_size("hst")
    cap = recv_rows.shape[-1]
    blocks = nodes // BLOCK
    norm_scale = 1.0 / math.sqrt(nodes * peers * groups)
    wide = 2 * cap

    gp, s1, lift_part = call(
        first_kernel,
        (
            shape((nodes, width), BF16),
            shape((groups, rank + 4 * width // groups, BLOCK), BF16),
            shape((rank, width), F32),
        ),
        [SMEM] * 4 + [VMEM] * 7,
        (cross_rows, cross_cols, cross_ids, cross_counts, grad_out, preact, feats, neigh_agg,
         cross_coords, lift, tile_values),
        [pltpu.VMEM((blocks, rank, BLOCK), BF16), pltpu.VMEM((groups, rank, BLOCK), F32)],
        flops=100_000_000,
    )
    s1 = lax.all_to_all(s1, "hst", split_axis=0, concat_axis=0, tiled=True)
    columns = blocks + peers * cap // BLOCK
    base, bnd = call(
        inner_kernel,
        (shape((nodes, width), F32), shape((peers, cap, width), F32)),
        [SMEM] * 4 + [VMEM] * 4,
        (tile_rows, tile_cols, tile_ids, send_counts, gp, w_neigh, w_self, tile_values),
        [pltpu.VMEM((blocks, BLOCK, width), BF16), pltpu.VMEM((columns, BLOCK, width), F32)],
        flops=350_000_000,
    )
    coords, s2 = call(
        second_kernel,
        (shape((nodes, rank), BF16), shape((peers * wide, width), BF16)),
        [VMEM] * 5,
        (s1, cross_recv_rows.reshape(groups, BLOCK), feats, lift_part, bnd),
        [pltpu.VMEM((2, peers * wide, BLOCK), F32)],
        flops=50_000_000,
    )
    s2 = lax.all_to_all(
        s2.reshape(peers, wide, width), "dev", split_axis=0, concat_axis=0, tiled=True
    ).reshape(peers * wide, width)
    recv = jnp.concatenate(
        [recv_rows.reshape(peers, cap), jnp.full((peers, cap), -1, jnp.int32)], axis=1
    ).reshape(1, peers * wide)
    (s3,) = call(third_kernel, (shape((groups, 8, BLOCK), F32),), [VMEM], (s2,), flops=10_000_000)
    s3 = lax.all_to_all(s3, "hst", split_axis=0, concat_axis=0, tiled=True)
    (grad_feats,) = call(
        feats_kernel,
        (shape((nodes, width), BF16),),
        [VMEM] * 5,
        (s2, recv, base, coords, proj),
        flops=150_000_000,
    )
    (s4,) = call(fourth_kernel, (shape((peers, 24, BLOCK), BF16),), [VMEM], (s3,))
    s4 = lax.all_to_all(s4, "dev", split_axis=0, concat_axis=0, tiled=True)
    grad_self, grad_neigh, grad_lift, grad_proj = call(
        lambda *refs: last_kernel(norm_scale, *refs),
        (
            shape((width, width), F32),
            shape((width, width), F32),
            shape((rank, width), F32),
            shape((width, rank), F32),
        ),
        [VMEM],
        (s4,),
        [pltpu.VMEM((peers * 24, BLOCK), F32)],
    )
    return (grad_feats, grad_self, grad_neigh, grad_lift, grad_proj)


def solution(mesh):
    both = ("hst", "dev")
    row, cube = P(both, None), P(both, None, None)
    placed = (
        (row,) * 5 + (P(),) * 4 + (cube,) + (row,) * 7 + (cube,) + (row,) + (cube,)
    )
    return jax.shard_map(
        body,
        mesh=mesh,
        in_specs=placed,
        out_specs=(row, P(), P(), P(), P()),
        check_vma=False,
    )
```

time: 365 us -> 97.6 us (0.27)
  waiting for transfers between devices: 268 us -> 24.4 us
  blocking collectives: 0 us -> 37.9 us
  other arithmetic: 27.5 us -> 0 us
  local copies, waits for them, and re-layouts: 22.1 us -> 8.08 us
  between operations: 14.3 us -> 0.84 us
  matrix products: 9.11 us -> 0 us
  Pallas kernels: 0 us -> 7.08 us
    psum x1 -> x0, waiting for transfers between devices: 264 us -> none  [body(): lax.psum((grad_self, grad_neigh, grad_lift, grad_proj), ('hst', 'dev'))]
    all_to_all x0 -> x2, blocking collectives: none -> 37.9 us  [the longest x1 28.7 us: body(): lax.all_to_all(s2.reshape(peers, wide, width), 'dev', split_axis=0, conca...]
    all_to_all x2, waiting for transfers between devices: 4.49 us -> 24.4 us  [the longest x1 12.6 us: body(): s4 = lax.all_to_all(s4, 'dev', split_axis=0, concat_axis=0, tiled=True)]
    scatter-add x6 -> x0, other arithmetic: 15.3 us -> none  [the longest x1 6.05 us: body(): coords = jnp.zeros((node_rows, rank_width), jnp.float32).at[cross_recv_ro...]
    gather x8 -> x0, local copies, waits for them, and re-layouts: 13.3 us -> none  [the longest x4 8.96 us: advance(): tile_vals[index_part]]
    dot_general x12 -> x0, matrix products: 9.11 us -> none  [the longest x4 4.14 us: advance(): jnp.einsum('tij,tif->tjf', tile_vals[index_part], pieces[row_part], prefe...]
    pallas_call x0 -> x7, Pallas kernels: none -> 7.08 us  [call(): pl.pallas_call(kernel, out_shape=tuple(outs), in_specs=specs, out_specs=t...]
    unnamed x6 -> x0, other arithmetic: 5.95 us -> none
  transfers between devices with their start and end apart: 3 -> 2, of which waited for: 2 -> 2; matrix products, arithmetic and copies ran while one was open for 10% -> 0% of each run, Pallas kernels for 0% -> 3%
where the time goes in v1:
time: 97.6 us; the launch traced here: 96.9 us
  blocking collectives  37.9 us (39%)
  waiting for transfers between devices  24.4 us (25%)
  starting transfers between devices  18.6 us (19%)
  local copies, waits for them, and re-layouts  8.08 us (8%)
  Pallas kernels  7.08 us (7%)
    all_to_all x1, blocking collectives, body(): lax.all_to_all(s2.reshape(peers, wide, width), 'dev', split_axis=0, conca...  28.7 us
    all_to_all x1, waiting for transfers between devices, body(): s4 = lax.all_to_all(s4, 'dev', split_axis=0, concat_axis=0, tiled=True)  12.6 us
    all_to_all x1, waiting for transfers between devices, body(): s1 = lax.all_to_all(s1, 'hst', split_axis=0, concat_axis=0, tiled=True)  11.8 us
    all_to_all x1, starting transfers between devices, body(): s1 = lax.all_to_all(s1, 'hst', split_axis=0, concat_axis=0, tiled=True)  11 us
    all_to_all x1, blocking collectives, body(): s3 = lax.all_to_all(s3, 'hst', split_axis=0, concat_axis=0, tiled=True)  9.24 us
    unnamed x46, local copies, waits for them, and re-layouts  7.99 us
    all_to_all x1, starting transfers between devices, body(): s4 = lax.all_to_all(s4, 'dev', split_axis=0, concat_axis=0, tiled=True)  7.56 us
    pallas_call x7, Pallas kernels, call(): pl.pallas_call(kernel, out_shape=tuple(outs), in_specs=specs, out_specs=t...  7.08 us
  transfers between devices with their start and end apart: 2, of which 2 were waited for; matrix products, arithmetic and copies ran while one was open for 0% of the time, Pallas kernels for 3%

profile of v1, /device:TPU:1, one launch (start us, length us, event | category | flops | bytes accessed | tf_op | source)
XLA Modules:
  0.0 96.9 jit_solution(17646282630185549225)
XLA Ops:
  0.6 0.0 copy-start.9
  0.6 0.0 copy-start.11
  0.7 0.0 copy-start.12
  0.7 0.0 copy-start.13
  0.7 0.0 copy-start.14
  0.7 0.9 copy.29.cross_coords
  1.6 0.0 copy-done.9
  1.6 0.0 copy-done.11
  1.6 0.0 copy-done.12
  1.6 0.0 copy-done.13
  1.6 0.0 copy-done.14
  1.6 0.0 copy-start
  1.6 1.2 %copy-done = bf16[32,128,128]{2,1,0:T(8,128)(2,1)S(1)} copy-done((bf16[32,128,128]{2,1,0:T(8,128)(2,1)S(1)}, bf16[32,128,128]{2,1,0:T(8,128)(2,1)}, u32[]{:S(2)}) %copy-start) | copy-done | bytes 1048600
  2.9 0.9 copy-done.2
  3.8 0.9 copy-done.4
  4.7 0.9 copy-done.5
  5.6 0.9 copy-done.6
  6.5 1.9 %shard_map.227 = (bf16[256,256]{1,0:T(8,128)(2,1)S(1)}, bf16[8,192,128]{2,1,0:T(8,128)(2,1)}, f32[64,256]{1,0:T(8,128)S(1)}) custom-call(s32[1,8]{1,0:T(1,128)S(1)} %copy-done.11, s32[1,8]{1,0:T(1,128)S(1)} %copy-done.12, s32[1,8]{1,0:T(1,128)S(1)} %copy-done.13, s32[1,8]{1,0:T(1,128)S(1)} %copy-done.14, bf16[256,256]{1,0:T(8,128)(2,1)S(1)} %copy-done.4, ...), custom_call_target="tpu_custom_call" | custom-call | flops 100000000 | bytes 2228352 | tf_op jit(solution)/shard_map/pallas_call | solution.py:32
  8.3 11.0 %all-to-all-start = ((bf16[8,192,128]{2,1,0:T(8,128)(2,1)}), bf16[8,192,128]{2,1,0:T(8,128)(2,1)S(1)}, u32[]{:S(2)}, u32[]{:S(2)}) async-start(bf16[8,192,128]{2,1,0:T(8,128)(2,1)} %get-tuple-element.16), calls=%async_computation | async-start | bytes 786432 | tf_op jit(solution)/shard_map/all_to_all | solution.py:239
  19.4 0.0 copy-start.16
  19.4 0.0 copy-start.17
  19.4 0.0 copy-done.1
  19.4 0.0 copy-done.7
  19.4 0.0 copy-done.8
  19.4 0.0 copy-done.18
  19.4 0.6 copy-done.15
  20.0 0.0 copy-done.16
  20.0 0.0 copy-done.17
  20.0 1.7 %shard_map.228 = (f32[256,256]{1,0:T(8,128)S(1)}, f32[64,8,256]{2,1,0:T(8,128)S(1)}) custom-call(s32[1,32]{1,0:T(1,128)S(1)} %copy-done.15, s32[1,32]{1,0:T(1,128)S(1)} %copy-done.16, s32[1,32]{1,0:T(1,128)S(1)} %copy-done.17, s32[1,64]{1,0:T(1,128)S(1)} %copy-done.18, bf16[256,256]{1,0:T(8,128)(2,1)S(1)} %get-tuple-element.18.gp, ...), custom_call_target="tpu_custom_call" | custom-call | flops 350000000 | bytes 2228864 | tf_op jit(solution)/shard_map/pallas_call | solution.py:32
  21.7 0.0 copy-start.10
  21.7 11.8 %all-to-all-done.s1 = bf16[8,192,128]{2,1,0:T(8,128)(2,1)S(1)} async-done(((bf16[8,192,128]{2,1,0:T(8,128)(2,1)}), bf16[8,192,128]{2,1,0:T(8,128)(2,1)S(1)}, u32[]{:S(2)}, u32[]{:S(2)}) %all-to-all-start) | async-done | bytes 393248 | tf_op jit(solution)/shard_map/all_to_all | solution.py:239
  33.5 0.0 copy-done.3
  33.5 0.0 copy-done.10
  33.5 0.6 shard_map.229
  34.2 28.7 %all_to_all.20 = bf16[64,16,256]{2,1,0:T(8,128)(2,1)S(1)} all-to-all(bf16[64,16,256]{2,1,0:T(8,128)(2,1)S(1)} %bitcast.6), channel_id=1, replica_groups=mesh['hst'=8,'dev'=64] {'dev'}, dimensions={0} | all-to-all | bytes 1048576 | tf_op jit(solution)/shard_map/all_to_all | solution.py:257
  62.8 0.2 shard_map.231
  63.0 9.2 %all_to_all.21.s3 = f32[8,8,128]{2,1,0:T(8,128)S(1)} all-to-all(f32[8,8,128]{2,1,0:T(8,128)S(1)} %shard_map.231), channel_id=1, replica_groups=mesh['hst'=8,'dev'=64] {'hst'}, dimensions={0} | all-to-all | bytes 65536 | tf_op jit(solution)/shard_map/all_to_all | solution.py:264
  72.3 0.8 shard_map.232
  73.1 7.6 %all-to-all-start.3 = ((bf16[64,24,128]{2,1,0:T(8,128)(2,1)}), bf16[64,24,128]{2,1,0:T(8,128)(2,1)S(1)}, u32[]{:S(2)}, u32[]{:S(2)}) async-start(bf16[64,24,128]{2,1,0:T(8,128)(2,1)} %shard_map.232), calls=%async_computation.3 | async-start | bytes 786432 | tf_op jit(solution)/shard_map/all_to_all | solution.py:273
  80.6 0.1 copy.33
  80.7 0.0 copy-start.19
  80.7 0.1 reshape.29.recv
  80.8 0.7 copy-done.19
  81.5 0.1 copy.31.proj
  81.6 1.0 %shard_map.230 = bf16[256,256]{1,0:T(8,128)(2,1)} custom-call(bf16[1024,256]{1,0:T(8,128)(2,1)S(1)} %bitcast.5, s32[1,1024]{1,0:T(1,128)S(1)} %reshape.29.recv, f32[256,256]{1,0:T(8,128)S(1)} %get-tuple-element.21.base, bf16[256,64]{1,0:T(8,128)(2,1)S(1)} %get-tuple-element.22.coords, bf16[256,64]{1,0:T(8,128)(2,1)S(1)} %copy.31.proj), custom_call_target="tpu_custom_call" | custom-call | flops 150000000 | bytes 987136 | tf_op jit(solution)/shard_map/pallas_call | solution.py:32
  82.6 12.6 %all-to-all-done.3.refs_0_ = bf16[64,24,128]{2,1,0:T(8,128)(2,1)S(1)} async-done(((bf16[64,24,128]{2,1,0:T(8,128)(2,1)}), bf16[64,24,128]{2,1,0:T(8,128)(2,1)S(1)}, u32[]{:S(2)}, u32[]{:S(2)}) %all-to-all-start.3) | async-done | bytes 393248 | tf_op jit(solution)/shard_map/all_to_all | solution.py:273
  95.2 1.0 %shard_map.233 = (f32[256,256]{1,0:T(8,128)}, f32[256,256]{1,0:T(8,128)}, f32[64,256]{1,0:T(8,128)}, f32[256,64]{1,0:T(8,128)S(1)}) custom-call(bf16[64,24,128]{2,1,0:T(8,128)(2,1)S(1)} %all-to-all-done.3.refs_0_), custom_call_target="tpu_custom_call" | custom-call | bytes 1048576 | tf_op jit(solution)/shard_map/pallas_call | solution.py:32
  96.2 0.7 copy.32
  (13 shorter events, 0.0 us)
Async XLA Ops:
  0.6 1.0 copy-start.9
  0.6 1.0 copy-start.11
  0.7 1.0 copy-start.12
  0.7 1.0 copy-start.13
  0.7 1.0 copy-start.14
  1.6 1.2 %copy-start = (bf16[32,128,128]{2,1,0:T(8,128)(2,1)S(1)}, bf16[32,128,128]{2,1,0:T(8,128)(2,1)}, u32[]{:S(2)}) copy-start(bf16[32,128,128]{2,1,0:T(8,128)(2,1)} %tiles.3) | copy-start | bytes 3145732
  2.9 0.9 copy-start.2
  3.8 0.9 copy-start.4
  4.7 0.9 copy-start.5
  5.6 0.9 copy-start.6
  6.5 12.9 %copy-start.1 = (bf16[32,128,128]{2,1,0:T(8,128)(2,1)S(1)}, bf16[32,128,128]{2,1,0:T(8,128)(2,1)}, u32[]{:S(2)}) copy-start(bf16[32,128,128]{2,1,0:T(8,128)(2,1)} %tiles.3) | copy-start | bytes 3145732
  8.3 11.1 %copy-start.7 = (bf16[256,256]{1,0:T(8,128)(2,1)S(1)}, bf16[256,256]{1,0:T(8,128)(2,1)}, u32[]{:S(2)}) copy-start(bf16[256,256]{1,0:T(8,128)(2,1)} %w_neigh.1) | copy-start | bytes 393220
  8.3 11.1 %copy-start.8 = (bf16[256,256]{1,0:T(8,128)(2,1)S(1)}, bf16[256,256]{1,0:T(8,128)(2,1)}, u32[]{:S(2)}) copy-start(bf16[256,256]{1,0:T(8,128)(2,1)} %w_self.1) | copy-start | bytes 393220
  8.3 11.1 %copy-start.18 = (s32[1,64]{1,0:T(1,128)S(1)}, s32[1,64]{1,0:T(1,128)}, u32[]{:S(2)}) copy-start(s32[1,64]{1,0:T(1,128)} %counts.1) | copy-start | bytes 772
  8.3 25.2 %all-to-all-start = ((bf16[8,192,128]{2,1,0:T(8,128)(2,1)}), bf16[8,192,128]{2,1,0:T(8,128)(2,1)S(1)}, u32[]{:S(2)}, u32[]{:S(2)}) async-start(bf16[8,192,128]{2,1,0:T(8,128)(2,1)} %get-tuple-element.16), calls=%async_computation | async-start | bytes 786432 | tf_op jit(solution)/shard_map/all_to_all | solution.py:239
  19.4 0.7 copy-start.15
  19.4 0.7 copy-start.16
  19.4 0.7 copy-start.17
  20.0 13.5 %copy-start.3 = (bf16[256,256]{1,0:T(8,128)(2,1)S(1)}, bf16[256,256]{1,0:T(8,128)(2,1)}, u32[]{:S(2)}) copy-start(bf16[256,256]{1,0:T(8,128)(2,1)} %feats.3) | copy-start | bytes 393220
  21.7 11.8 %copy-start.10 = (s32[1,8,128]{2,1,0:T(8,128)S(1)}, s32[1,8,128]{2,1,0:T(8,128)}, u32[]{:S(2)}) copy-start(s32[1,8,128]{2,1,0:T(8,128)} %param.39) | copy-start | bytes 12292
  73.1 7.6 %copy-start.20 = (s32[1,64,8]{1,2,0:T(8,128)S(1)}, s32[1,64,8]{1,2,0:T(8,128)}, u32[]{:S(2)}) copy-start(s32[1,64,8]{1,2,0:T(8,128)} %param.37) | copy-start | bytes 6148
  73.1 22.2 %all-to-all-start.3 = ((bf16[64,24,128]{2,1,0:T(8,128)(2,1)}), bf16[64,24,128]{2,1,0:T(8,128)(2,1)S(1)}, u32[]{:S(2)}, u32[]{:S(2)}) async-start(bf16[64,24,128]{2,1,0:T(8,128)(2,1)} %shard_map.232), calls=%async_computation.3 | async-start | bytes 786432 | tf_op jit(solution)/shard_map/all_to_all | solution.py:273
  80.7 0.8 copy-start.19

commit v2 on v1

v2 whole, which is shorter than its diff:
```python
import math

import jax
import jax.numpy as jnp
from jax import lax
from jax.experimental import pallas as pl
from jax.experimental.pallas import tpu as pltpu
from jax.sharding import PartitionSpec as P

F32 = jnp.float32
BF16 = jnp.bfloat16
BLOCK = 128

VMEM = pl.BlockSpec(memory_space=pltpu.VMEM)
SMEM = pl.BlockSpec(memory_space=pltpu.SMEM)
HBM = pl.BlockSpec(memory_space=pltpu.HBM)


def dot_nn(a, b):
    return jnp.dot(a, b, preferred_element_type=F32)


def dot_nt(a, b):
    return lax.dot_general(a, b, (((1,), (1,)), ((), ())), preferred_element_type=F32)


def dot_tn(a, b):
    return lax.dot_general(a, b, (((0,), (0,)), ((), ())), preferred_element_type=F32)


def call(kernel, outs, specs, args, scratch=(), flops=0, limit=40):
    nbytes = sum(math.prod(o.shape) * o.dtype.itemsize for o in list(outs) + list(args))
    return pl.pallas_call(
        kernel,
        out_shape=tuple(outs),
        in_specs=specs,
        out_specs=tuple(VMEM for _ in outs),
        scratch_shapes=list(scratch),
        compiler_params=pltpu.CompilerParams(vmem_limit_bytes=limit * 1024 * 1024),
        cost_estimate=pl.CostEstimate(flops=flops, bytes_accessed=nbytes, transcendentals=0),
    )(*args)


def shape(dims, dtype):
    return jax.ShapeDtypeStruct(dims, dtype)


def first_kernel(
    xrow_in, xcol_in, xid_in, xcount_in, grad_in, preact_in, lift_in, tiles_in, feats_in, agg_in, coords_in,
    gp_out, s1_out, lift_out,
    xrow, xcol, xid, xcount, grad, preact, lift, tiles, feats, agg, cross, cg, acc, sems,
):
    groups = acc.shape[0]
    rank = acc.shape[1]
    pairs = (
        (grad_in, grad), (preact_in, preact), (lift_in, lift), (xrow_in, xrow), (xcol_in, xcol),
        (xid_in, xid), (xcount_in, xcount), (tiles_in, tiles), (feats_in, feats), (agg_in, agg),
        (coords_in, cross),
    )
    copies = [
        pltpu.make_async_copy(source, target, sems.at[i])
        for i, (source, target) in enumerate(pairs)
    ]
    for copy in copies:
        copy.start()
    for copy in copies[:3]:
        copy.wait()
    gp = jnp.where(preact[...].astype(F32) > 0, grad[...].astype(F32), 0.0).astype(BF16)
    gp_out[...] = gp
    cgt = dot_nt(lift[...], gp).astype(BF16)
    for b in range(cg.shape[0]):
        cg[b] = cgt[:, b * BLOCK : (b + 1) * BLOCK]
    acc[...] = jnp.zeros_like(acc)
    for copy in copies[3:8]:
        copy.wait()
    for t in range(xrow.shape[1]):
        col = xcol[0, t]
        acc[col] += dot_nn(cg[xrow[0, t]], tiles[xid[0, t]])
    slot = lax.broadcasted_iota(jnp.int32, (rank, BLOCK), 1)
    for j in range(groups):
        s1_out[j, 0:rank, :] = jnp.where(slot < xcount[0, j], acc[j], 0.0).astype(BF16)
    at = rank
    for copy, source in ((copies[8], feats), (copies[9], agg)):
        copy.wait()
        part = dot_tn(source[...], gp).astype(BF16)
        step = part.shape[0] // groups
        for j in range(groups):
            rows = part[j * step : (j + 1) * step]
            s1_out[j, at : at + step, :] = rows[:, :BLOCK]
            s1_out[j, at + step : at + 2 * step, :] = rows[:, BLOCK:]
        at += 2 * step
    copies[10].wait()
    lift_out[...] = dot_nn(cross[...], gp)


def inner_kernel(trow, tcol, tid, counts, gp, w_neigh, w_self, tiles, base_out, bnd_out, ng, acc):
    cap = bnd_out.shape[1]
    blocks = ng.shape[0]
    own = dot_nt(gp[...], w_self[...])
    grad = dot_nt(gp[...], w_neigh[...]).astype(BF16)
    for b in range(blocks):
        ng[b] = grad[b * BLOCK : (b + 1) * BLOCK]
    acc[...] = jnp.zeros_like(acc)
    for t in range(trow.shape[1]):
        col = tcol[0, t]
        acc[col] += dot_tn(tiles[tid[0, t]], ng[trow[0, t]])
    for b in range(blocks):
        base_out[b * BLOCK : (b + 1) * BLOCK, :] = own[b * BLOCK : (b + 1) * BLOCK] + acc[b]
    slot = lax.broadcasted_iota(jnp.int32, (cap, acc.shape[2]), 0)
    per_block = BLOCK // cap
    for q in range(bnd_out.shape[0]):
        rows = acc[blocks + q // per_block, (q % per_block) * cap : (q % per_block + 1) * cap, :]
        bnd_out[q] = jnp.where(slot < counts[0, q], rows, 0.0)


def second_kernel(s1, xrecv, feats, lift_part, bnd, coords_out, s2_out, scr):
    groups = s1.shape[0]
    rank = lift_part.shape[0]
    peers = bnd.shape[0]
    cap = bnd.shape[1]
    nodes = feats.shape[0]
    wide = 3 * cap
    row = lax.broadcasted_iota(jnp.int32, (nodes, BLOCK), 0)
    total = None
    for g in range(groups):
        hot = jnp.where(row == xrecv[g : g + 1, :], 1.0, 0.0).astype(BF16)
        term = dot_nt(s1[g, 0:rank, :], hot)
        total = term if total is None else total + term
    coords_t = total.astype(BF16)
    coords_out[...] = total.T.astype(BF16)
    proj_t = dot_nn(coords_t, feats[...])
    summed = s1[0, rank:, :].astype(F32)
    for g in range(1, groups):
        summed = summed + s1[g, rank:, :].astype(F32)
    for q in range(peers):
        scr[q * wide : q * wide + cap, :] = bnd[q, :, :BLOCK]
        scr[q * wide + cap : q * wide + 2 * cap, :] = bnd[q, :, BLOCK:]
    low = proj_t - proj_t.astype(BF16).astype(F32)
    pieces = [summed[:peers], summed[peers:]]
    for value in (proj_t, lift_part[...], low):
        pieces += [value[:, :BLOCK], value[:, BLOCK:]]
    for at, piece in enumerate(pieces):
        scr[pl.ds(2 * cap + at, peers, stride=wide), :] = piece
    s2_out[...] = scr[...].astype(BF16)


def third_kernel(s2, s3_out):
    parts = [s2[q, 16:24, :].astype(F32) for q in range(s2.shape[0])]
    while len(parts) > 1:
        parts = [parts[i] + parts[i + 1] for i in range(0, len(parts), 2)]
    sums = parts[0]
    proj = sums[2:4] + sums[6:8]
    low = proj - proj.astype(BF16).astype(F32)
    share = jnp.concatenate([sums[0:2], proj, sums[4:6], low], axis=0).astype(BF16)
    for j in range(s3_out.shape[0]):
        s3_out[j] = share


def feats_kernel(s2, recv, base, coords, proj_t, out):
    nodes = base.shape[0]
    row = lax.broadcasted_iota(jnp.int32, (nodes, recv.shape[1]), 0)
    for half in range(2):
        lanes = slice(half * BLOCK, (half + 1) * BLOCK)
        hot = jnp.where(row == recv[half : half + 1, :], 1.0, 0.0).astype(BF16)
        value = base[:, lanes] + dot_nn(hot, s2[...]) + dot_nn(coords[...], proj_t[:, lanes])
        out[:, lanes] = value.astype(BF16)


def fourth_kernel(s3, s4_out, scr):
    for j in range(s3.shape[0]):
        scr[j * 8 : (j + 1) * 8, :] = s3[j].astype(F32)
    peers = s3.shape[0]
    side = peers // 8
    pieces = [scr[pl.ds(at, peers, stride=8), :] for at in range(2)]

    def over_groups(at):
        total = scr[pl.ds(at, side, stride=8), :]
        for g in range(1, 8):
            total = total + scr[pl.ds(g * side * 8 + at, side, stride=8), :]
        return total

    for at in range(2):
        pieces.append(over_groups(2 + at) + over_groups(6 + at))
    for at in range(2):
        pieces.append(over_groups(4 + at))
    share = jnp.concatenate(pieces, axis=0).astype(BF16)
    for j in range(s4_out.shape[0]):
        s4_out[j] = share


def last_kernel(norm_scale, s4, self_out, neigh_out, lift_out, proj_out, square, flat):
    groups = 8
    for j in range(s4.shape[0]):
        value = s4[j].astype(F32) * norm_scale
        first = 16 * (j // 2) + j % 2
        for kind in range(2):
            for g in range(groups):
                at = 64 * kind + 8 * g
                square[2 * kind + first // 32, pl.ds(32 * g + first % 32, 8, stride=2), :] = value[
                    at : at + 8
                ]
        for part in range(4):
            at = 128 + 8 * part
            flat[part, pl.ds(first, 8, stride=2), :] = value[at : at + 8]
    for h in range(2):
        lanes = slice(h * BLOCK, (h + 1) * BLOCK)
        self_out[:, lanes] = square[h]
        neigh_out[:, lanes] = square[2 + h]
        proj_out[:, lanes] = flat[h]
        lift_out[:, lanes] = flat[2 + h]


def device_groups(inner):
    sizes = (("z", 8), ("x", 4), ("y", 8), ("core", 2))
    lists = {}
    for z in range(8):
        for x in range(4):
            for y in range(8):
                for core in range(2):
                    place = {"z": z, "x": x, "y": y, "core": core}
                    key = tuple(place[name] for name, _ in sizes if name not in inner)
                    lists.setdefault(key, []).append(((z * 4 + x) * 8 + y) * 2 + core)
    return [lists[key] for key in sorted(lists)]


def body(
    feats,
    grad_out,
    preact,
    neigh_agg,
    cross_coords,
    w_self,
    w_neigh,
    proj,
    lift,
    tile_values,
    tile_rows,
    tile_cols,
    tile_ids,
    cross_rows,
    cross_cols,
    cross_ids,
    send_counts,
    recv_rows,
    cross_counts,
    cross_recv_rows,
):
    nodes, width = feats.shape
    rank = proj.shape[1]
    peers = lax.axis_size("dev")
    groups = lax.axis_size("hst")
    cap = recv_rows.shape[-1]
    blocks = nodes // BLOCK
    norm_scale = 1.0 / math.sqrt(nodes * peers * groups)
    wide = 3 * cap
    both = ("hst", "dev")

    first_args = (
        cross_rows, cross_cols, cross_ids, cross_counts, grad_out, preact, lift, tile_values,
        feats, neigh_agg, cross_coords.T,
    )
    gp, s1, lift_part = call(
        first_kernel,
        (
            shape((nodes, width), BF16),
            shape((groups, rank + 4 * width // groups, BLOCK), BF16),
            shape((rank, width), F32),
        ),
        [HBM] * 11,
        first_args,
        [pltpu.SMEM(v.shape, v.dtype) for v in first_args[:4]]
        + [pltpu.VMEM(v.shape, v.dtype) for v in first_args[4:]]
        + [
            pltpu.VMEM((blocks, rank, BLOCK), BF16),
            pltpu.VMEM((groups, rank, BLOCK), F32),
            pltpu.SemaphoreType.DMA((11,)),
        ],
        flops=100_000_000,
        limit=60,
    )
    s1 = lax.all_to_all(s1, "hst", split_axis=0, concat_axis=0, tiled=True)
    columns = blocks + peers * cap // BLOCK
    base, bnd = call(
        inner_kernel,
        (shape((nodes, width), F32), shape((peers, cap, width), F32)),
        [SMEM] * 4 + [VMEM] * 4,
        (tile_rows, tile_cols, tile_ids, send_counts, gp, w_neigh, w_self, tile_values),
        [pltpu.VMEM((blocks, BLOCK, width), BF16), pltpu.VMEM((columns, BLOCK, width), F32)],
        flops=350_000_000,
    )
    coords, s2 = call(
        second_kernel,
        (shape((nodes, rank), BF16), shape((peers * wide, BLOCK), BF16)),
        [VMEM] * 5,
        (s1, cross_recv_rows.reshape(groups, BLOCK), feats, lift_part, bnd),
        [pltpu.VMEM((peers * wide, BLOCK), F32)],
        flops=50_000_000,
    )
    s2 = lax.all_to_all(
        s2.reshape(peers, wide, BLOCK), "dev", split_axis=0, concat_axis=0, tiled=True
    )
    slots = recv_rows.reshape(peers, cap)
    recv = jnp.stack(
        [
            jnp.pad(slots, ((0, 0), (at * cap, (2 - at) * cap)), constant_values=-1).reshape(-1)
            for at in range(2)
        ]
    )
    (s3,) = call(third_kernel, (shape((64, 8, BLOCK), BF16),), [VMEM], (s2,), flops=10_000_000)
    s3 = lax.all_to_all(
        s3, both, split_axis=0, concat_axis=0, tiled=True, axis_index_groups=device_groups(("z", "y"))
    )
    (grad_feats,) = call(
        feats_kernel,
        (shape((nodes, width), BF16),),
        [VMEM] * 5,
        (s2.reshape(peers * wide, BLOCK), recv, base, coords, proj.T),
        flops=150_000_000,
    )
    (s4,) = call(
        fourth_kernel,
        (shape((8, 160, BLOCK), BF16),),
        [VMEM],
        (s3,),
        [pltpu.VMEM((512, BLOCK), F32)],
    )
    s4 = lax.all_to_all(
        s4, both, split_axis=0, concat_axis=0, tiled=True,
        axis_index_groups=device_groups(("x", "core")),
    )
    grad_self, grad_neigh, grad_lift, grad_proj = call(
        lambda *refs: last_kernel(norm_scale, *refs),
        (
            shape((width, width), F32),
            shape((width, width), F32),
            shape((rank, width), F32),
            shape((rank, width), F32),
        ),
        [VMEM],
        (s4,),
        [pltpu.VMEM((4, width, BLOCK), F32), pltpu.VMEM((4, rank, BLOCK), F32)],
    )
    return (grad_feats, grad_self, grad_neigh, grad_lift, grad_proj.T)


def solution(mesh):
    both = ("hst", "dev")
    row, cube = P(both, None), P(both, None, None)
    placed = (
        (row,) * 5 + (P(),) * 4 + (cube,) + (row,) * 7 + (cube,) + (row,) + (cube,)
    )
    return jax.shard_map(
        body,
        mesh=mesh,
        in_specs=placed,
        out_specs=(row, P(), P(), P(), P()),
        check_vma=False,
    )
```

time: 97.6 us -> 88 us (0.902)
  blocking collectives: 37.9 us -> 26 us
  local copies, waits for them, and re-layouts: 8.08 us -> 1.64 us
  waiting for transfers between devices: 24.4 us -> 28.2 us
  starting transfers between devices: 18.6 us -> 22 us
  Pallas kernels: 7.08 us -> 8.82 us
    all_to_all x2 -> x1, blocking collectives: 37.9 us -> 26 us  [body(): lax.all_to_all(s2.reshape(peers, wide, BLOCK), 'dev', split_axis=0, conca...]
    unnamed x46 -> x27, local copies, waits for them, and re-layouts: 7.99 us -> 1.39 us
    all_to_all x1 -> x2, waiting for transfers between devices: 12.6 us -> 16.4 us  [the longest x1 11.4 us: body(): lax.all_to_all(s3, both, split_axis=0, concat_axis=0, tiled=True, axis_in...]
    all_to_all x1 -> x2, starting transfers between devices: 7.56 us -> 11 us  [the longest x1 6.01 us: body(): lax.all_to_all(s4, both, split_axis=0, concat_axis=0, tiled=True, axis_in...]
    pallas_call x7, Pallas kernels: 7.08 us -> 8.82 us  [call(): pl.pallas_call(kernel, out_shape=tuple(outs), in_specs=specs, out_specs=t...]
  transfers between devices with their start and end apart: 2 -> 3, of which waited for: 2 -> 3; matrix products, arithmetic and copies ran while one was open for 0% -> 0% of each run, Pallas kernels for 3% -> 3%
where the time goes in v2:
time: 88 us; the launch traced here: 87.5 us
  waiting for transfers between devices  28.2 us (32%)
  blocking collectives  26 us (30%)
  starting transfers between devices  22 us (25%)
  Pallas kernels  8.82 us (10%)
  local copies, waits for them, and re-layouts  1.64 us (2%)
    all_to_all x1, blocking collectives, body(): lax.all_to_all(s2.reshape(peers, wide, BLOCK), 'dev', split_axis=0, conca...  26 us
    all_to_all x1, waiting for transfers between devices, body(): s1 = lax.all_to_all(s1, 'hst', split_axis=0, concat_axis=0, tiled=True)  11.8 us
    all_to_all x1, waiting for transfers between devices, body(): lax.all_to_all(s3, both, split_axis=0, concat_axis=0, tiled=True, axis_in...  11.4 us
    all_to_all x1, starting transfers between devices, body(): s1 = lax.all_to_all(s1, 'hst', split_axis=0, concat_axis=0, tiled=True)  11 us
    pallas_call x7, Pallas kernels, call(): pl.pallas_call(kernel, out_shape=tuple(outs), in_specs=specs, out_specs=t...  8.82 us
    all_to_all x1, starting transfers between devices, body(): lax.all_to_all(s4, both, split_axis=0, concat_axis=0, tiled=True, axis_in...  6.01 us
    all_to_all x1, starting transfers between devices, body(): lax.all_to_all(s3, both, split_axis=0, concat_axis=0, tiled=True, axis_in...  5.02 us
    all_to_all x1, waiting for transfers between devices, body(): lax.all_to_all(s4, both, split_axis=0, concat_axis=0, tiled=True, axis_in...  4.93 us
  transfers between devices with their start and end apart: 3, of which 3 were waited for; matrix products, arithmetic and copies ran while one was open for 0% of the time, Pallas kernels for 3%

profile of v2, /device:TPU:1, one launch (start us, length us, event | category | flops | bytes accessed | tf_op | source)
XLA Modules:
  0.0 87.5 jit_solution(7668639952718210276)
XLA Ops:
  0.6 0.0 copy-start
  0.6 3.1 %shard_map.227 = (bf16[256,256]{1,0:T(8,128)(2,1)}, bf16[8,192,128]{2,1,0:T(8,128)(2,1)}, f32[64,256]{1,0:T(8,128)}) custom-call(s32[1,8]{1,0:T(1,128)} %xrow_in.1, s32[1,8]{1,0:T(1,128)} %xcol_in.1, s32[1,8]{1,0:T(1,128)} %xid_in.1, s32[1,8]{1,0:T(1,128)} %xcount_in.1, bf16[256,256]{1,0:T(8,128)(2,1)} %grad_in.1, bf16[256,256]{1,0:T(8,128)(2,1)} %preact_in.1, ...), custom_call_target="tpu_custom_call" | custom-call | flops 100000000 | bytes 2228352 | tf_op jit(solution)/shard_map/pallas_call | solution.py:33
  3.7 0.0 copy-start.2
  3.7 0.0 copy-start.3
  3.8 0.0 copy-start.4
  3.8 0.0 copy-start.11
  3.8 11.0 %all-to-all-start = ((bf16[8,192,128]{2,1,0:T(8,128)(2,1)}), bf16[8,192,128]{2,1,0:T(8,128)(2,1)S(1)}, u32[]{:S(2)}, u32[]{:S(2)}) async-start(bf16[8,192,128]{2,1,0:T(8,128)(2,1)} %get-tuple-element.16), calls=%async_computation | async-start | bytes 786432 | tf_op jit(solution)/shard_map/all_to_all | solution.py:281
  14.8 0.0 copy-start.8
  14.8 0.0 copy-start.9
  14.8 0.0 copy-start.10
  14.8 0.0 copy-done
  14.8 0.0 copy-done.2
  14.8 0.0 copy-done.3
  14.8 0.0 copy-done.4
  14.9 0.0 copy-done.11
  14.9 0.6 copy-done.8
  15.4 0.0 copy-done.9
  15.5 0.0 copy-done.10
  15.5 0.0 copy-start.1
  15.5 0.0 copy-start.5
  15.5 1.7 %shard_map.228 = (f32[256,256]{1,0:T(8,128)S(1)}, f32[64,8,256]{2,1,0:T(8,128)S(1)}) custom-call(s32[1,32]{1,0:T(1,128)S(1)} %copy-done.8, s32[1,32]{1,0:T(1,128)S(1)} %copy-done.9, s32[1,32]{1,0:T(1,128)S(1)} %copy-done.10, s32[1,64]{1,0:T(1,128)S(1)} %copy-done.11, bf16[256,256]{1,0:T(8,128)(2,1)S(1)} %copy-done.4, bf16[256,256]{1,0:T(8,128)(2,1)S(1)} %copy-done.2, ...), custom_call_target="tpu_custom_call" | custom-call | flops 350000000 | bytes 2228864 | tf_op jit(solution)/shard_map/pallas_call | solution.py:33
  17.2 0.0 copy-start.7
  17.2 11.8 %all-to-all-done.s1 = bf16[8,192,128]{2,1,0:T(8,128)(2,1)S(1)} async-done(((bf16[8,192,128]{2,1,0:T(8,128)(2,1)}), bf16[8,192,128]{2,1,0:T(8,128)(2,1)S(1)}, u32[]{:S(2)}, u32[]{:S(2)}) %all-to-all-start) | async-done | bytes 393248 | tf_op jit(solution)/shard_map/all_to_all | solution.py:281
  29.0 0.0 copy-done.1
  29.0 0.0 copy-done.5
  29.0 0.0 copy-done.7
  29.0 0.5 shard_map.229
  29.5 26.0 %all_to_all.20.s2 = bf16[64,24,128]{2,1,0:T(8,128)(2,1)S(1)} all-to-all(bf16[64,24,128]{2,1,0:T(8,128)(2,1)S(1)} %bitcast.8), channel_id=1, replica_groups=mesh['hst'=8,'dev'=64] {'dev'}, dimensions={0} | all-to-all | bytes 786432 | tf_op jit(solution)/shard_map/all_to_all | solution.py:299
  55.5 0.7 shard_map.231
  56.1 0.0 copy-start.12
  56.2 5.0 %all-to-all-start.2 = ((bf16[64,8,128]{2,1,0:T(8,128)(2,1)}), bf16[64,8,128]{2,1,0:T(8,128)(2,1)S(1)}, u32[]{:S(2)}, u32[]{:S(2)}) async-start(bf16[64,8,128]{2,1,0:T(8,128)(2,1)} %shard_map.231), calls=%async_computation.2 | async-start | bytes 262144 | tf_op jit(solution)/shard_map/all_to_all | solution.py:310
  61.2 0.0 copy-done.12
  61.2 0.1 copy.29
  61.3 11.4 %all-to-all-done.2.s3 = bf16[64,8,128]{2,1,0:T(8,128)(2,1)S(1)} async-done(((bf16[64,8,128]{2,1,0:T(8,128)(2,1)}), bf16[64,8,128]{2,1,0:T(8,128)(2,1)S(1)}, u32[]{:S(2)}, u32[]{:S(2)}) %all-to-all-start.2) | async-done | bytes 131104 | tf_op jit(solution)/shard_map/all_to_all | solution.py:310
  72.7 0.8 shard_map.232
  73.5 6.0 %all-to-all-start.3 = ((bf16[8,160,128]{2,1,0:T(8,128)(2,1)}), bf16[8,160,128]{2,1,0:T(8,128)(2,1)S(1)}, u32[]{:S(2)}, u32[]{:S(2)}) async-start(bf16[8,160,128]{2,1,0:T(8,128)(2,1)} %shard_map.232), calls=%async_computation.3 | async-start | bytes 655360 | tf_op jit(solution)/shard_map/all_to_all | solution.py:327
  79.5 0.1 fusion
  79.6 0.1 stack_reshape.6
  79.7 0.0 copy-start.6
  79.7 0.1 stack_reshape.7
  79.8 0.6 copy-done.6
  80.4 1.3 %shard_map.230 = bf16[256,256]{1,0:T(8,128)(2,1)} custom-call(bf16[1536,128]{1,0:T(8,128)(2,1)S(1)} %bitcast.7, s32[2,1536]{1,0:T(2,128)S(1)} %pad_add_fusion.recv, f32[256,256]{1,0:T(8,128)S(1)} %get-tuple-element.21.base, bf16[256,64]{1,0:T(8,128)(2,1)S(1)} %get-tuple-element.22.coords, bf16[64,256]{1,0:T(8,128)(2,1)S(1)} %bitcast.9), custom_call_target="tpu_custom_call" | custom-call | flops 150000000 | bytes 864256 | tf_op jit(solution)/shard_map/pallas_call | solution.py:33
  81.7 4.9 %all-to-all-done.3.refs_0_ = bf16[8,160,128]{2,1,0:T(8,128)(2,1)S(1)} async-done(((bf16[8,160,128]{2,1,0:T(8,128)(2,1)}), bf16[8,160,128]{2,1,0:T(8,128)(2,1)S(1)}, u32[]{:S(2)}, u32[]{:S(2)}) %all-to-all-start.3) | async-done | bytes 327712 | tf_op jit(solution)/shard_map/all_to_all | solution.py:327
  86.6 0.9 shard_map.233
  (1 shorter events, 0.0 us)
Async XLA Ops:
  0.6 14.2 %copy-start = (bf16[32,128,128]{2,1,0:T(8,128)(2,1)S(1)}, bf16[32,128,128]{2,1,0:T(8,128)(2,1)}, u32[]{:S(2)}) copy-start(bf16[32,128,128]{2,1,0:T(8,128)(2,1)} %tiles.1) | copy-start | bytes 3145732
  3.7 11.1 %copy-start.2 = (bf16[256,256]{1,0:T(8,128)(2,1)S(1)}, bf16[256,256]{1,0:T(8,128)(2,1)}, u32[]{:S(2)}) copy-start(bf16[256,256]{1,0:T(8,128)(2,1)} %w_neigh.1) | copy-start | bytes 393220
  3.7 11.1 %copy-start.3 = (bf16[256,256]{1,0:T(8,128)(2,1)S(1)}, bf16[256,256]{1,0:T(8,128)(2,1)}, u32[]{:S(2)}) copy-start(bf16[256,256]{1,0:T(8,128)(2,1)} %w_self.1) | copy-start | bytes 393220
  3.8 11.1 %copy-start.4 = (bf16[256,256]{1,0:T(8,128)(2,1)S(1)}, bf16[256,256]{1,0:T(8,128)(2,1)}, u32[]{:S(2)}) copy-start(bf16[256,256]{1,0:T(8,128)(2,1)} %get-tuple-element.18.gp) | copy-start | bytes 393220
  3.8 11.1 %copy-start.11 = (s32[1,64]{1,0:T(1,128)S(1)}, s32[1,64]{1,0:T(1,128)}, u32[]{:S(2)}) copy-start(s32[1,64]{1,0:T(1,128)} %counts.1) | copy-start | bytes 772
  3.8 25.2 %all-to-all-start = ((bf16[8,192,128]{2,1,0:T(8,128)(2,1)}), bf16[8,192,128]{2,1,0:T(8,128)(2,1)S(1)}, u32[]{:S(2)}, u32[]{:S(2)}) async-start(bf16[8,192,128]{2,1,0:T(8,128)(2,1)} %get-tuple-element.16), calls=%async_computation | async-start | bytes 786432 | tf_op jit(solution)/shard_map/all_to_all | solution.py:281
  14.8 0.7 copy-start.8
  14.8 0.7 copy-start.9
  14.8 0.7 copy-start.10
  15.5 13.5 %copy-start.1 = (bf16[256,256]{1,0:T(8,128)(2,1)S(1)}, bf16[256,256]{1,0:T(8,128)(2,1)}, u32[]{:S(2)}) copy-start(bf16[256,256]{1,0:T(8,128)(2,1)} %feats.1) | copy-start | bytes 393220
  15.5 13.5 %copy-start.5 = (f32[64,256]{1,0:T(8,128)S(1)}, f32[64,256]{1,0:T(8,128)}, u32[]{:S(2)}) copy-start(f32[64,256]{1,0:T(8,128)} %get-tuple-element.17.lift_part) | copy-start | bytes 196612
  17.2 11.8 %copy-start.7 = (s32[1,8,128]{2,1,0:T(8,128)S(1)}, s32[1,8,128]{2,1,0:T(8,128)}, u32[]{:S(2)}) copy-start(s32[1,8,128]{2,1,0:T(8,128)} %param.39) | copy-start | bytes 12292
  56.1 5.0 %copy-start.12 = (s32[1,64,8]{1,2,0:T(8,128)S(1)}, s32[1,64,8]{1,2,0:T(8,128)}, u32[]{:S(2)}) copy-start(s32[1,64,8]{1,2,0:T(8,128)} %param.37) | copy-start | bytes 6148
  56.2 16.6 %all-to-all-start.2 = ((bf16[64,8,128]{2,1,0:T(8,128)(2,1)}), bf16[64,8,128]{2,1,0:T(8,128)(2,1)S(1)}, u32[]{:S(2)}, u32[]{:S(2)}) async-start(bf16[64,8,128]{2,1,0:T(8,128)(2,1)} %shard_map.231), calls=%async_computation.2 | async-start | bytes 262144 | tf_op jit(solution)/shard_map/all_to_all | solution.py:310
  73.5 13.1 %all-to-all-start.3 = ((bf16[8,160,128]{2,1,0:T(8,128)(2,1)}), bf16[8,160,128]{2,1,0:T(8,128)(2,1)S(1)}, u32[]{:S(2)}, u32[]{:S(2)}) async-start(bf16[8,160,128]{2,1,0:T(8,128)(2,1)} %shard_map.232), calls=%async_computation.3 | async-start | bytes 655360 | tf_op jit(solution)/shard_map/all_to_all | solution.py:327
  79.7 0.8 copy-start.6

commit v3 on v2

--- a/solution.py
+++ b/solution.py
@@ -45,17 +45,20 @@
     return jax.ShapeDtypeStruct(dims, dtype)
 
 
+def masked(grad, preact):
+    return jnp.where(preact[...].astype(F32) > 0, grad[...].astype(F32), 0.0).astype(BF16)
+
+
 def first_kernel(
-    xrow_in, xcol_in, xid_in, xcount_in, grad_in, preact_in, lift_in, tiles_in, feats_in, agg_in, coords_in,
-    gp_out, s1_out, lift_out,
-    xrow, xcol, xid, xcount, grad, preact, lift, tiles, feats, agg, cross, cg, acc, sems,
+    xrow_in, xcol_in, xid_in, xcount_in, grad_in, preact_in, lift_in, tiles_in, feats_in, agg_in,
+    s1_out,
+    xrow, xcol, xid, xcount, grad, preact, lift, tiles, feats, agg, cg, acc, sems,
 ):
     groups = acc.shape[0]
     rank = acc.shape[1]
     pairs = (
         (grad_in, grad), (preact_in, preact), (lift_in, lift), (xrow_in, xrow), (xcol_in, xcol),
         (xid_in, xid), (xcount_in, xcount), (tiles_in, tiles), (feats_in, feats), (agg_in, agg),
-        (coords_in, cross),
     )
     copies = [
         pltpu.make_async_copy(source, target, sems.at[i])
@@ -63,25 +66,14 @@
     ]
     for copy in copies:
         copy.start()
-    for copy in copies[:3]:
+    for copy in copies:
         copy.wait()
-    gp = jnp.where(preact[...].astype(F32) > 0, grad[...].astype(F32), 0.0).astype(BF16)
-    gp_out[...] = gp
+    gp = masked(grad, preact)
     cgt = dot_nt(lift[...], gp).astype(BF16)
     for b in range(cg.shape[0]):
         cg[b] = cgt[:, b * BLOCK : (b + 1) * BLOCK]
-    acc[...] = jnp.zeros_like(acc)
-    for copy in copies[3:8]:
-        copy.wait()
-    for t in range(xrow.shape[1]):
-        col = xcol[0, t]
-        acc[col] += dot_nn(cg[xrow[0, t]], tiles[xid[0, t]])
-    slot = lax.broadcasted_iota(jnp.int32, (rank, BLOCK), 1)
-    for j in range(groups):
-        s1_out[j, 0:rank, :] = jnp.where(slot < xcount[0, j], acc[j], 0.0).astype(BF16)
     at = rank
-    for copy, source in ((copies[8], feats), (copies[9], agg)):
-        copy.wait()
+    for source in (feats, agg):
         part = dot_tn(source[...], gp).astype(BF16)
         step = part.shape[0] // groups
         for j in range(groups):
@@ -89,15 +81,24 @@
             s1_out[j, at : at + step, :] = rows[:, :BLOCK]
             s1_out[j, at + step : at + 2 * step, :] = rows[:, BLOCK:]
         at += 2 * step
-    copies[10].wait()
-    lift_out[...] = dot_nn(cross[...], gp)
-
-
-def inner_kernel(trow, tcol, tid, counts, gp, w_neigh, w_self, tiles, base_out, bnd_out, ng, acc):
+    acc[...] = jnp.zeros_like(acc)
+    for t in range(xrow.shape[1]):
+        acc[xcol[0, t]] += dot_nn(cg[xrow[0, t]], tiles[xid[0, t]])
+    slot = lax.broadcasted_iota(jnp.int32, (rank, BLOCK), 1)
+    for j in range(groups):
+        s1_out[j, 0:rank, :] = jnp.where(slot < xcount[0, j], acc[j], 0.0).astype(BF16)
+
+
+def inner_kernel(
+    trow, tcol, tid, counts, grad_out, preact, cross, w_neigh, w_self, tiles,
+    base_out, bnd_out, lift_out, ng, acc,
+):
     cap = bnd_out.shape[1]
     blocks = ng.shape[0]
-    own = dot_nt(gp[...], w_self[...])
-    grad = dot_nt(gp[...], w_neigh[...]).astype(BF16)
+    gp = masked(grad_out, preact)
+    lift_out[...] = dot_nn(cross[...], gp)
+    own = dot_nt(gp, w_self[...])
+    grad = dot_nt(gp, w_neigh[...]).astype(BF16)
     for b in range(blocks):
         ng[b] = grad[b * BLOCK : (b + 1) * BLOCK]
     acc[...] = jnp.zeros_like(acc)
@@ -257,34 +258,43 @@
 
     first_args = (
         cross_rows, cross_cols, cross_ids, cross_counts, grad_out, preact, lift, tile_values,
-        feats, neigh_agg, cross_coords.T,
-    )
-    gp, s1, lift_part = call(
+        feats, neigh_agg,
+    )
+    (s1,) = call(
         first_kernel,
-        (
-            shape((nodes, width), BF16),
-            shape((groups, rank + 4 * width // groups, BLOCK), BF16),
-            shape((rank, width), F32),
-        ),
-        [HBM] * 11,
+        (shape((groups, rank + 4 * width // groups, BLOCK), BF16),),
+        [HBM] * 10,
         first_args,
         [pltpu.SMEM(v.shape, v.dtype) for v in first_args[:4]]
         + [pltpu.VMEM(v.shape, v.dtype) for v in first_args[4:]]
         + [
             pltpu.VMEM((blocks, rank, BLOCK), BF16),
             pltpu.VMEM((groups, rank, BLOCK), F32),
-            pltpu.SemaphoreType.DMA((11,)),
+            pltpu.SemaphoreType.DMA((10,)),
         ],
         flops=100_000_000,
         limit=60,
     )
     s1 = lax.all_to_all(s1, "hst", split_axis=0, concat_axis=0, tiled=True)
+    slots = recv_rows.reshape(peers, cap)
+    recv = jnp.stack(
+        [
+            jnp.pad(slots, ((0, 0), (at * cap, (2 - at) * cap)), constant_values=-1).reshape(-1)
+            for at in range(2)
+        ]
+    )
+    recv, sweep_rows = lax.optimization_barrier((recv, tile_rows))
     columns = blocks + peers * cap // BLOCK
-    base, bnd = call(
+    base, bnd, lift_part = call(
         inner_kernel,
-        (shape((nodes, width), F32), shape((peers, cap, width), F32)),
-        [SMEM] * 4 + [VMEM] * 4,
-        (tile_rows, tile_cols, tile_ids, send_counts, gp, w_neigh, w_self, tile_values),
+        (
+            shape((nodes, width), F32),
+            shape((peers, cap, width), F32),
+            shape((rank, width), F32),
+        ),
+        [SMEM] * 4 + [VMEM] * 6,
+        (sweep_rows, tile_cols, tile_ids, send_counts, grad_out, preact, cross_coords.T,
+         w_neigh, w_self, tile_values),
         [pltpu.VMEM((blocks, BLOCK, width), BF16), pltpu.VMEM((columns, BLOCK, width), F32)],
         flops=350_000_000,
     )
@@ -299,13 +309,6 @@
     s2 = lax.all_to_all(
         s2.reshape(peers, wide, BLOCK), "dev", split_axis=0, concat_axis=0, tiled=True
     )
-    slots = recv_rows.reshape(peers, cap)
-    recv = jnp.stack(
-        [
-            jnp.pad(slots, ((0, 0), (at * cap, (2 - at) * cap)), constant_values=-1).reshape(-1)
-            for at in range(2)
-        ]
-    )
     (s3,) = call(third_kernel, (shape((64, 8, BLOCK), BF16),), [VMEM], (s2,), flops=10_000_000)
     s3 = lax.all_to_all(
         s3, both, split_axis=0, concat_axis=0, tiled=True, axis_index_groups=device_groups(("z", "y"))
@@ -317,6 +320,7 @@
         (s2.reshape(peers * wide, BLOCK), recv, base, coords, proj.T),
         flops=150_000_000,
     )
+    s3, grad_feats = lax.optimization_barrier((s3, grad_feats))
     (s4,) = call(
         fourth_kernel,
         (shape((8, 160, BLOCK), BF16),),

time: 88 us -> 87.1 us (0.990)
  blocking collectives: 26 us -> 39.3 us
  waiting for transfers between devices: 28.2 us -> 21.7 us
  starting transfers between devices: 22 us -> 16 us
  Pallas kernels: 8.82 us -> 7.81 us
    all_to_all x0 -> x1, blocking collectives: none -> 13.3 us  [body(): lax.all_to_all(s4, both, split_axis=0, concat_axis=0, tiled=True, axis_in...]
    all_to_all x1 -> x0, starting transfers between devices: 6.01 us -> none  [body(): lax.all_to_all(s4, both, split_axis=0, concat_axis=0, tiled=True, axis_in...]
    all_to_all x1 -> x0, waiting for transfers between devices: 4.93 us -> none  [body(): lax.all_to_all(s4, both, split_axis=0, concat_axis=0, tiled=True, axis_in...]
    all_to_all x1, waiting for transfers between devices: 11.4 us -> 10.3 us  [body(): lax.all_to_all(s3, both, split_axis=0, concat_axis=0, tiled=True, axis_in...]
    pallas_call x7, Pallas kernels: 8.82 us -> 7.81 us  [call(): pl.pallas_call(kernel, out_shape=tuple(outs), in_specs=specs, out_specs=t...]
  transfers between devices with their start and end apart: 3 -> 2, of which waited for: 3 -> 2; matrix products, arithmetic and copies ran while one was open for 0% -> 0% of each run, Pallas kernels for 3% -> 3%
where the time goes in v3:
time: 87.1 us; the launch traced here: 86.7 us
  blocking collectives  39.3 us (45%)
  waiting for transfers between devices  21.7 us (25%)
  starting transfers between devices  16 us (18%)
  Pallas kernels  7.81 us (9%)
  local copies, waits for them, and re-layouts  1.04 us (1%)
    all_to_all x1, blocking collectives, body(): lax.all_to_all(s2.reshape(peers, wide, BLOCK), 'dev', split_axis=0, conca...  26 us
    all_to_all x1, blocking collectives, body(): lax.all_to_all(s4, both, split_axis=0, concat_axis=0, tiled=True, axis_in...  13.3 us
    all_to_all x1, waiting for transfers between devices, body(): s1 = lax.all_to_all(s1, 'hst', split_axis=0, concat_axis=0, tiled=True)  11.4 us
    all_to_all x1, starting transfers between devices, body(): s1 = lax.all_to_all(s1, 'hst', split_axis=0, concat_axis=0, tiled=True)  11 us
    all_to_all x1, waiting for transfers between devices, body(): lax.all_to_all(s3, both, split_axis=0, concat_axis=0, tiled=True, axis_in...  10.3 us
    pallas_call x7, Pallas kernels, call(): pl.pallas_call(kernel, out_shape=tuple(outs), in_specs=specs, out_specs=t...  7.81 us
    all_to_all x1, starting transfers between devices, body(): lax.all_to_all(s3, both, split_axis=0, concat_axis=0, tiled=True, axis_in...  5.02 us
  transfers between devices with their start and end apart: 2, of which 2 were waited for; matrix products, arithmetic and copies ran while one was open for 0% of the time, Pallas kernels for 3%

profile of v3, /device:TPU:1, one launch (start us, length us, event | category | flops | bytes accessed | tf_op | source)
XLA Modules:
  0.0 86.7 jit_solution(13562981329957750811)
XLA Ops:
  0.6 0.0 copy-start
  0.6 2.8 %shard_map.227 = bf16[8,192,128]{2,1,0:T(8,128)(2,1)} custom-call(s32[1,8]{1,0:T(1,128)} %xrow_in.1, s32[1,8]{1,0:T(1,128)} %xcol_in.1, s32[1,8]{1,0:T(1,128)} %xid_in.1, s32[1,8]{1,0:T(1,128)} %xcount_in.1, bf16[256,256]{1,0:T(8,128)(2,1)} %grad_out.1, bf16[256,256]{1,0:T(8,128)(2,1)} %preact.1, bf16[64,256]{1,0:T(8,128)(2,1)} %lift_in.1, ...), custom_call_target="tpu_custom_call" | custom-call | flops 100000000 | bytes 1998976 | tf_op jit(solution)/shard_map/pallas_call | solution.py:33
  3.4 0.0 copy-start.13
  3.4 0.0 copy-start.2
  3.5 0.0 copy-start.4
  3.5 0.0 copy-start.5
  3.5 11.0 %all-to-all-start = ((bf16[8,192,128]{2,1,0:T(8,128)(2,1)}), bf16[8,192,128]{2,1,0:T(8,128)(2,1)S(1)}, u32[]{:S(2)}, u32[]{:S(2)}) async-start(bf16[8,192,128]{2,1,0:T(8,128)(2,1)} %shard_map.227), calls=%async_computation | async-start | bytes 786432 | tf_op jit(solution)/shard_map/all_to_all | solution.py:278
  14.5 0.0 copy-start.1
  14.5 0.0 copy-done.13
  14.5 0.1 copy.29
  14.6 0.1 fusion
  14.7 0.1 stack_reshape.6
  14.8 0.0 copy-start.7
  14.8 0.0 copy-start.12
  14.8 0.1 stack_reshape.7
  14.9 0.0 copy-start.9
  14.9 0.0 copy-start.10
  14.9 0.0 copy-start.11
  14.9 0.0 copy-done
  15.0 0.0 copy-done.2
  15.0 0.0 copy-done.4
  15.0 0.0 copy-done.5
  15.0 0.4 copy-done.1
  15.4 0.1 copy-done.7
  15.5 0.0 copy-done.12
  15.5 0.0 copy-done.9
  15.6 0.0 copy-done.10
  15.6 0.0 copy-done.11
  15.6 0.0 copy-start.3
  15.6 1.7 %shard_map.228 = (f32[256,256]{1,0:T(8,128)S(1)}, f32[64,8,256]{2,1,0:T(8,128)S(1)}, f32[64,256]{1,0:T(8,128)S(1)}) custom-call(s32[1,32]{1,0:T(1,128)S(1)} %copy-done.9, s32[1,32]{1,0:T(1,128)S(1)} %copy-done.10, s32[1,32]{1,0:T(1,128)S(1)} %copy-done.11, s32[1,64]{1,0:T(1,128)S(1)} %copy-done.12, bf16[256,256]{1,0:T(8,128)(2,1)S(1)} %copy-done.1, ...), custom_call_target="tpu_custom_call" | custom-call | flops 350000000 | bytes 2458240 | tf_op jit(solution)/shard_map/pallas_call | solution.py:33
  17.3 0.0 copy-start.8
  17.3 11.4 %all-to-all-done.s1 = bf16[8,192,128]{2,1,0:T(8,128)(2,1)S(1)} async-done(((bf16[8,192,128]{2,1,0:T(8,128)(2,1)}), bf16[8,192,128]{2,1,0:T(8,128)(2,1)S(1)}, u32[]{:S(2)}, u32[]{:S(2)}) %all-to-all-start) | async-done | bytes 393248 | tf_op jit(solution)/shard_map/all_to_all | solution.py:278
  28.7 0.0 copy-done.3
  28.7 0.0 copy-done.8
  28.7 0.5 shard_map.229
  29.2 26.0 %all_to_all.20.s2 = bf16[64,24,128]{2,1,0:T(8,128)(2,1)S(1)} all-to-all(bf16[64,24,128]{2,1,0:T(8,128)(2,1)S(1)} %bitcast.8), channel_id=1, replica_groups=mesh['hst'=8,'dev'=64] {'dev'}, dimensions={0} | all-to-all | bytes 786432 | tf_op jit(solution)/shard_map/all_to_all | solution.py:309
  55.2 0.7 shard_map.230
  55.8 0.0 copy-start.6
  55.8 5.0 %all-to-all-start.2 = ((bf16[64,8,128]{2,1,0:T(8,128)(2,1)}), bf16[64,8,128]{2,1,0:T(8,128)(2,1)S(1)}, u32[]{:S(2)}, u32[]{:S(2)}) async-start(bf16[64,8,128]{2,1,0:T(8,128)(2,1)} %shard_map.230), calls=%async_computation.2 | async-start | bytes 262144 | tf_op jit(solution)/shard_map/all_to_all | solution.py:313
  60.9 0.0 copy-done.6
  60.9 1.3 %shard_map.231 = bf16[256,256]{1,0:T(8,128)(2,1)} custom-call(bf16[1536,128]{1,0:T(8,128)(2,1)S(1)} %bitcast.7, s32[2,1536]{1,0:T(2,128)S(1)} %pad_add_fusion.recv, f32[256,256]{1,0:T(8,128)S(1)} %get-tuple-element.23.base, bf16[256,64]{1,0:T(8,128)(2,1)S(1)} %get-tuple-element.24.coords, bf16[64,256]{1,0:T(8,128)(2,1)S(1)} %bitcast.9), custom_call_target="tpu_custom_call" | custom-call | flops 150000000 | bytes 864256 | tf_op jit(solution)/shard_map/pallas_call | solution.py:33
  62.1 10.3 %all-to-all-done.2.s3 = bf16[64,8,128]{2,1,0:T(8,128)(2,1)S(1)} async-done(((bf16[64,8,128]{2,1,0:T(8,128)(2,1)}), bf16[64,8,128]{2,1,0:T(8,128)(2,1)S(1)}, u32[]{:S(2)}, u32[]{:S(2)}) %all-to-all-start.2) | async-done | bytes 131104 | tf_op jit(solution)/shard_map/all_to_all | solution.py:313
  72.4 0.1 shard_map.232
  72.5 13.3 %all_to_all.21.refs_0_ = bf16[8,160,128]{2,1,0:T(8,128)(2,1)S(1)} all-to-all(bf16[8,160,128]{2,1,0:T(8,128)(2,1)S(1)} %shard_map.232), channel_id=1, replica_groups={{0,1,16,17,32,33,48,49},{2,3,18,19,34,35,50,51},{4,5,20,21,36,37,52,53}..., dimensions={0} | all-to-all | bytes 655360 | tf_op jit(solution)/shard_map/all_to_all | solution.py:331
  85.8 0.9 %shard_map.233 = (f32[256,256]{1,0:T(8,128)}, f32[256,256]{1,0:T(8,128)}, f32[64,256]{1,0:T(8,128)}, f32[64,256]{1,0:T(8,128)}) custom-call(bf16[8,160,128]{2,1,0:T(8,128)(2,1)S(1)} %all_to_all.21.refs_0_), custom_call_target="tpu_custom_call" | custom-call | bytes 983040 | tf_op jit(solution)/shard_map/pallas_call | solution.py:33
  (1 shorter events, 0.0 us)
Async XLA Ops:
  0.6 14.3 %copy-start = (bf16[32,128,128]{2,1,0:T(8,128)(2,1)S(1)}, bf16[32,128,128]{2,1,0:T(8,128)(2,1)}, u32[]{:S(2)}) copy-start(bf16[32,128,128]{2,1,0:T(8,128)(2,1)} %tiles.1) | copy-start | bytes 3145732
  3.4 11.1 %copy-start.13 = (s32[1,64,8]{1,2,0:T(8,128)S(1)}, s32[1,64,8]{1,2,0:T(8,128)}, u32[]{:S(2)}) copy-start(s32[1,64,8]{1,2,0:T(8,128)} %param.37) | copy-start | bytes 6148
  3.4 11.5 %copy-start.2 = (bf16[256,256]{1,0:T(8,128)(2,1)S(1)}, bf16[256,256]{1,0:T(8,128)(2,1)}, u32[]{:S(2)}) copy-start(bf16[256,256]{1,0:T(8,128)(2,1)} %preact.1) | copy-start | bytes 393220
  3.5 11.5 %copy-start.4 = (bf16[256,256]{1,0:T(8,128)(2,1)S(1)}, bf16[256,256]{1,0:T(8,128)(2,1)}, u32[]{:S(2)}) copy-start(bf16[256,256]{1,0:T(8,128)(2,1)} %w_neigh.1) | copy-start | bytes 393220
  3.5 11.5 %copy-start.5 = (bf16[256,256]{1,0:T(8,128)(2,1)S(1)}, bf16[256,256]{1,0:T(8,128)(2,1)}, u32[]{:S(2)}) copy-start(bf16[256,256]{1,0:T(8,128)(2,1)} %w_self.1) | copy-start | bytes 393220
  3.5 25.2 %all-to-all-start = ((bf16[8,192,128]{2,1,0:T(8,128)(2,1)}), bf16[8,192,128]{2,1,0:T(8,128)(2,1)S(1)}, u32[]{:S(2)}, u32[]{:S(2)}) async-start(bf16[8,192,128]{2,1,0:T(8,128)(2,1)} %shard_map.227), calls=%async_computation | async-start | bytes 786432 | tf_op jit(solution)/shard_map/all_to_all | solution.py:278
  14.5 0.9 %copy-start.1 = (bf16[256,256]{1,0:T(8,128)(2,1)S(1)}, bf16[256,256]{1,0:T(8,128)(2,1)}, u32[]{:S(2)}) copy-start(bf16[256,256]{1,0:T(8,128)(2,1)} %grad_out.1) | copy-start | bytes 393220
  14.8 0.8 copy-start.7
  14.8 0.8 copy-start.12
  14.9 0.7 copy-start.9
  14.9 0.7 copy-start.10
  14.9 0.7 copy-start.11
  15.6 13.1 %copy-start.3 = (bf16[256,256]{1,0:T(8,128)(2,1)S(1)}, bf16[256,256]{1,0:T(8,128)(2,1)}, u32[]{:S(2)}) copy-start(bf16[256,256]{1,0:T(8,128)(2,1)} %feats.1) | copy-start | bytes 393220
  17.3 11.4 %copy-start.8 = (s32[1,8,128]{2,1,0:T(8,128)S(1)}, s32[1,8,128]{2,1,0:T(8,128)}, u32[]{:S(2)}) copy-start(s32[1,8,128]{2,1,0:T(8,128)} %param.39) | copy-start | bytes 12292
  55.8 5.0 %copy-start.6 = (bf16[256,64]{0,1:T(8,128)(2,1)S(1)}, bf16[256,64]{0,1:T(8,128)(2,1)}, u32[]{:S(2)}) copy-start(bf16[256,64]{0,1:T(8,128)(2,1)} %param.27) | copy-start | bytes 98308
  55.8 16.6 %all-to-all-start.2 = ((bf16[64,8,128]{2,1,0:T(8,128)(2,1)}), bf16[64,8,128]{2,1,0:T(8,128)(2,1)S(1)}, u32[]{:S(2)}, u32[]{:S(2)}) async-start(bf16[64,8,128]{2,1,0:T(8,128)(2,1)} %shard_map.230), calls=%async_computation.2 | async-start | bytes 262144 | tf_op jit(solution)/shard_map/all_to_all | solution.py:313

commit v4 on v3

--- a/solution.py
+++ b/solution.py
@@ -120,7 +120,7 @@
     peers = bnd.shape[0]
     cap = bnd.shape[1]
     nodes = feats.shape[0]
-    wide = 3 * cap
+    wide = 2 * cap + 6
     row = lax.broadcasted_iota(jnp.int32, (nodes, BLOCK), 0)
     total = None
     for g in range(groups):
@@ -136,25 +136,25 @@
     for q in range(peers):
         scr[q * wide : q * wide + cap, :] = bnd[q, :, :BLOCK]
         scr[q * wide + cap : q * wide + 2 * cap, :] = bnd[q, :, BLOCK:]
-    low = proj_t - proj_t.astype(BF16).astype(F32)
     pieces = [summed[:peers], summed[peers:]]
-    for value in (proj_t, lift_part[...], low):
+    for value in (proj_t, lift_part[...]):
         pieces += [value[:, :BLOCK], value[:, BLOCK:]]
     for at, piece in enumerate(pieces):
         scr[pl.ds(2 * cap + at, peers, stride=wide), :] = piece
     s2_out[...] = scr[...].astype(BF16)
 
 
-def third_kernel(s2, s3_out):
-    parts = [s2[q, 16:24, :].astype(F32) for q in range(s2.shape[0])]
-    while len(parts) > 1:
-        parts = [parts[i] + parts[i + 1] for i in range(0, len(parts), 2)]
-    sums = parts[0]
-    proj = sums[2:4] + sums[6:8]
-    low = proj - proj.astype(BF16).astype(F32)
-    share = jnp.concatenate([sums[0:2], proj, sums[4:6], low], axis=0).astype(BF16)
-    for j in range(s3_out.shape[0]):
-        s3_out[j] = share
+def third_kernel(s2, s3_out, scr):
+    peers = 64
+    wide = s2.shape[0] // peers
+    scr[...] = s2[...].astype(F32)
+    sums = [
+        jnp.sum(scr[pl.ds(wide - 6 + at, peers, stride=wide), :], axis=0, keepdims=True)
+        for at in range(6)
+    ]
+    share = jnp.concatenate(sums * 8, axis=0).astype(BF16)
+    for j in range(8):
+        s3_out[48 * j : 48 * (j + 1), :] = share
 
 
 def feats_kernel(s2, recv, base, coords, proj_t, out):
@@ -168,22 +168,15 @@
 
 
 def fourth_kernel(s3, s4_out, scr):
-    for j in range(s3.shape[0]):
-        scr[j * 8 : (j + 1) * 8, :] = s3[j].astype(F32)
-    peers = s3.shape[0]
+    scr[...] = s3[...].astype(F32)
+    peers = s3.shape[0] // 6
     side = peers // 8
-    pieces = [scr[pl.ds(at, peers, stride=8), :] for at in range(2)]
-
-    def over_groups(at):
-        total = scr[pl.ds(at, side, stride=8), :]
+    pieces = [scr[pl.ds(at, peers, stride=6), :] for at in range(2)]
+    for at in range(2, 6):
+        total = scr[pl.ds(at, side, stride=6), :]
         for g in range(1, 8):
-            total = total + scr[pl.ds(g * side * 8 + at, side, stride=8), :]
-        return total
-
-    for at in range(2):
-        pieces.append(over_groups(2 + at) + over_groups(6 + at))
-    for at in range(2):
-        pieces.append(over_groups(4 + at))
+            total = total + scr[pl.ds(g * side * 6 + at, side, stride=6), :]
+        pieces.append(total)
     share = jnp.concatenate(pieces, axis=0).astype(BF16)
     for j in range(s4_out.shape[0]):
         s4_out[j] = share
@@ -253,7 +246,7 @@
     cap = recv_rows.shape[-1]
     blocks = nodes // BLOCK
     norm_scale = 1.0 / math.sqrt(nodes * peers * groups)
-    wide = 3 * cap
+    wide = 2 * cap + 6
     both = ("hst", "dev")
 
     first_args = (
@@ -279,7 +272,7 @@
     slots = recv_rows.reshape(peers, cap)
     recv = jnp.stack(
         [
-            jnp.pad(slots, ((0, 0), (at * cap, (2 - at) * cap)), constant_values=-1).reshape(-1)
+            jnp.pad(slots, ((0, 0), (at * cap, wide - (at + 1) * cap)), constant_values=-1).reshape(-1)
             for at in range(2)
         ]
     )
@@ -307,17 +300,25 @@
         flops=50_000_000,
     )
     s2 = lax.all_to_all(
-        s2.reshape(peers, wide, BLOCK), "dev", split_axis=0, concat_axis=0, tiled=True
-    )
-    (s3,) = call(third_kernel, (shape((64, 8, BLOCK), BF16),), [VMEM], (s2,), flops=10_000_000)
+        s2.reshape(peers * wide // 2, 2, BLOCK), "dev", split_axis=0, concat_axis=0, tiled=True
+    ).reshape(peers * wide, BLOCK)
+    (s3,) = call(
+        third_kernel,
+        (shape((64 * 6, BLOCK), BF16),),
+        [VMEM],
+        (s2,),
+        [pltpu.VMEM((peers * wide, BLOCK), F32)],
+        flops=10_000_000,
+    )
     s3 = lax.all_to_all(
-        s3, both, split_axis=0, concat_axis=0, tiled=True, axis_index_groups=device_groups(("z", "y"))
-    )
+        s3.reshape(64 * 3, 2, BLOCK), both, split_axis=0, concat_axis=0, tiled=True,
+        axis_index_groups=device_groups(("z", "y")),
+    ).reshape(64 * 6, BLOCK)
     (grad_feats,) = call(
         feats_kernel,
         (shape((nodes, width), BF16),),
         [VMEM] * 5,
-        (s2.reshape(peers * wide, BLOCK), recv, base, coords, proj.T),
+        (s2, recv, base, coords, proj.T),
         flops=150_000_000,
     )
     s3, grad_feats = lax.optimization_barrier((s3, grad_feats))
@@ -326,7 +327,7 @@
         (shape((8, 160, BLOCK), BF16),),
         [VMEM],
         (s3,),
-        [pltpu.VMEM((512, BLOCK), F32)],
+        [pltpu.VMEM((64 * 6, BLOCK), F32)],
     )
     s4 = lax.all_to_all(
         s4, both, split_axis=0, concat_axis=0, tiled=True,

time: 87.1 us -> 85.8 us (0.985)
  blocking collectives: 39.3 us -> 38.4 us
  transfers between devices with their start and end apart: 2 -> 2, of which waited for: 2 -> 2; matrix products, arithmetic and copies ran while one was open for 0% -> 1% of each run, Pallas kernels for 3% -> 3%
where the time goes in v4:
time: 85.8 us; the launch traced here: 85.4 us
  blocking collectives  38.4 us (45%)
  waiting for transfers between devices  21.4 us (25%)
  starting transfers between devices  16 us (19%)
  Pallas kernels  7.74 us (9%)
  local copies, waits for them, and re-layouts  1.14 us (1%)
    all_to_all x1, blocking collectives, body(): lax.all_to_all(s2.reshape(peers * wide // 2, 2, BLOCK), 'dev', split_axis...  25.4 us
    all_to_all x1, blocking collectives, body(): lax.all_to_all(s4, both, split_axis=0, concat_axis=0, tiled=True, axis_in...  13 us
    all_to_all x1, waiting for transfers between devices, body(): s1 = lax.all_to_all(s1, 'hst', split_axis=0, concat_axis=0, tiled=True)  11.3 us
    all_to_all x1, starting transfers between devices, body(): s1 = lax.all_to_all(s1, 'hst', split_axis=0, concat_axis=0, tiled=True)  11 us
    all_to_all x1, waiting for transfers between devices, body(): lax.all_to_all(s3.reshape(64 * 3, 2, BLOCK), both, split_axis=0, concat_a...  10.1 us
    pallas_call x7, Pallas kernels, call(): pl.pallas_call(kernel, out_shape=tuple(outs), in_specs=specs, out_specs=t...  7.74 us
    all_to_all x1, starting transfers between devices, body(): lax.all_to_all(s3.reshape(64 * 3, 2, BLOCK), both, split_axis=0, concat_a...  4.94 us
  transfers between devices with their start and end apart: 2, of which 2 were waited for; matrix products, arithmetic and copies ran while one was open for 1% of the time, Pallas kernels for 3%

profile of v4, /device:TPU:1, one launch (start us, length us, event | category | flops | bytes accessed | tf_op | source)
XLA Modules:
  0.0 85.4 jit_solution(2561915661932093617)
XLA Ops:
  0.6 0.0 copy-start
  0.6 2.8 %shard_map.227 = bf16[8,192,128]{2,1,0:T(8,128)(2,1)} custom-call(s32[1,8]{1,0:T(1,128)} %xrow_in.1, s32[1,8]{1,0:T(1,128)} %xcol_in.1, s32[1,8]{1,0:T(1,128)} %xid_in.1, s32[1,8]{1,0:T(1,128)} %xcount_in.1, bf16[256,256]{1,0:T(8,128)(2,1)} %grad_out.1, bf16[256,256]{1,0:T(8,128)(2,1)} %preact.1, bf16[64,256]{1,0:T(8,128)(2,1)} %lift_in.1, ...), custom_call_target="tpu_custom_call" | custom-call | flops 100000000 | bytes 1998976 | tf_op jit(solution)/shard_map/pallas_call | solution.py:33
  3.4 0.0 copy-start.13
  3.4 0.0 copy-start.2
  3.5 0.0 copy-start.4
  3.5 0.0 copy-start.5
  3.5 11.0 %all-to-all-start = ((bf16[8,192,128]{2,1,0:T(8,128)(2,1)}), bf16[8,192,128]{2,1,0:T(8,128)(2,1)S(1)}, u32[]{:S(2)}, u32[]{:S(2)}) async-start(bf16[8,192,128]{2,1,0:T(8,128)(2,1)} %shard_map.227), calls=%async_computation | async-start | bytes 786432 | tf_op jit(solution)/shard_map/all_to_all | solution.py:271
  14.5 0.0 copy-start.1
  14.5 0.0 copy-done.13
  14.5 0.1 copy.29
  14.6 0.1 fusion
  14.7 0.1 stack_reshape.6
  14.8 0.0 copy-start.6
  14.8 0.0 copy-start.12
  14.8 0.1 stack_reshape.7
  15.0 0.0 copy-start.9
  15.0 0.0 copy-start.10
  15.0 0.0 copy-start.11
  15.0 0.0 copy-done
  15.0 0.0 copy-done.2
  15.1 0.0 copy-done.4
  15.1 0.0 copy-done.5
  15.1 0.3 copy-done.1
  15.4 0.2 copy-done.6
  15.6 0.0 copy-done.12
  15.6 0.1 copy-done.9
  15.7 0.0 copy-done.10
  15.7 0.0 copy-done.11
  15.7 0.0 copy-start.3
  15.7 1.7 %shard_map.228 = (f32[256,256]{1,0:T(8,128)S(1)}, f32[64,8,256]{2,1,0:T(8,128)S(1)}, f32[64,256]{1,0:T(8,128)S(1)}) custom-call(s32[1,32]{1,0:T(1,128)S(1)} %copy-done.9, s32[1,32]{1,0:T(1,128)S(1)} %copy-done.10, s32[1,32]{1,0:T(1,128)S(1)} %copy-done.11, s32[1,64]{1,0:T(1,128)S(1)} %copy-done.12, bf16[256,256]{1,0:T(8,128)(2,1)S(1)} %copy-done.1, ...), custom_call_target="tpu_custom_call" | custom-call | flops 350000000 | bytes 2458240 | tf_op jit(solution)/shard_map/pallas_call | solution.py:33
  17.4 0.0 copy-start.8
  17.4 11.3 %all-to-all-done.s1 = bf16[8,192,128]{2,1,0:T(8,128)(2,1)S(1)} async-done(((bf16[8,192,128]{2,1,0:T(8,128)(2,1)}), bf16[8,192,128]{2,1,0:T(8,128)(2,1)S(1)}, u32[]{:S(2)}, u32[]{:S(2)}) %all-to-all-start) | async-done | bytes 393248 | tf_op jit(solution)/shard_map/all_to_all | solution.py:271
  28.7 0.0 copy-done.3
  28.7 0.0 copy-done.8
  28.7 0.5 shard_map.229
  29.2 25.4 %all_to_all.20 = bf16[704,2,128]{2,1,0:T(2,128)(2,1)S(1)} all-to-all(bf16[704,2,128]{2,1,0:T(2,128)(2,1)S(1)} %bitcast.12), channel_id=1, replica_groups=mesh['hst'=8,'dev'=64] {'dev'}, dimensions={0} | all-to-all | bytes 720896 | tf_op jit(solution)/shard_map/all_to_all | solution.py:302
  54.5 0.7 shard_map.230
  55.2 0.0 copy-start.7
  55.2 4.9 %all-to-all-start.2 = ((bf16[192,2,128]{2,1,0:T(2,128)(2,1)}), bf16[192,2,128]{2,1,0:T(2,128)(2,1)S(1)}, u32[]{:S(2)}, u32[]{:S(2)}) async-start(bf16[192,2,128]{2,1,0:T(2,128)(2,1)} %bitcast.5), calls=%async_computation.2 | async-start | bytes 196608 | tf_op jit(solution)/shard_map/all_to_all | solution.py:313
  60.2 0.0 copy-done.7
  60.2 1.2 %shard_map.231 = bf16[256,256]{1,0:T(8,128)(2,1)} custom-call(bf16[1408,128]{1,0:T(8,128)(2,1)S(1)} %bitcast.10, s32[2,1408]{1,0:T(2,128)S(1)} %pad_add_fusion.recv, f32[256,256]{1,0:T(8,128)S(1)} %get-tuple-element.23.base, bf16[256,64]{1,0:T(8,128)(2,1)S(1)} %get-tuple-element.24.coords, bf16[64,256]{1,0:T(8,128)(2,1)S(1)} %bitcast.14), custom_call_target="tpu_custom_call" | custom-call | flops 150000000 | bytes 830464 | tf_op jit(solution)/shard_map/pallas_call | solution.py:33
  61.4 10.1 %all-to-all-done.2 = bf16[192,2,128]{2,1,0:T(2,128)(2,1)S(1)} async-done(((bf16[192,2,128]{2,1,0:T(2,128)(2,1)}), bf16[192,2,128]{2,1,0:T(2,128)(2,1)S(1)}, u32[]{:S(2)}, u32[]{:S(2)}) %all-to-all-start.2) | async-done | bytes 98336 | tf_op jit(solution)/shard_map/all_to_all | solution.py:313
  71.6 13.0 %all_to_all.21.refs_0_ = bf16[8,160,128]{2,1,0:T(8,128)(2,1)S(1)} all-to-all(bf16[8,160,128]{2,1,0:T(8,128)(2,1)S(1)} %shard_map.232), channel_id=1, replica_groups={{0,1,16,17,32,33,48,49},{2,3,18,19,34,35,50,51},{4,5,20,21,36,37,52,53}..., dimensions={0} | all-to-all | bytes 655360 | tf_op jit(solution)/shard_map/all_to_all | solution.py:332
  84.5 0.9 %shard_map.233 = (f32[256,256]{1,0:T(8,128)}, f32[256,256]{1,0:T(8,128)}, f32[64,256]{1,0:T(8,128)}, f32[64,256]{1,0:T(8,128)}) custom-call(bf16[8,160,128]{2,1,0:T(8,128)(2,1)S(1)} %all_to_all.21.refs_0_), custom_call_target="tpu_custom_call" | custom-call | bytes 983040 | tf_op jit(solution)/shard_map/pallas_call | solution.py:33
  (2 shorter events, 0.1 us)
Async XLA Ops:
  0.6 14.4 %copy-start = (bf16[32,128,128]{2,1,0:T(8,128)(2,1)S(1)}, bf16[32,128,128]{2,1,0:T(8,128)(2,1)}, u32[]{:S(2)}) copy-start(bf16[32,128,128]{2,1,0:T(8,128)(2,1)} %tiles.1) | copy-start | bytes 3145732
  3.4 11.1 %copy-start.13 = (s32[1,64,8]{1,2,0:T(8,128)S(1)}, s32[1,64,8]{1,2,0:T(8,128)}, u32[]{:S(2)}) copy-start(s32[1,64,8]{1,2,0:T(8,128)} %param.37) | copy-start | bytes 6148
  3.4 11.6 %copy-start.2 = (bf16[256,256]{1,0:T(8,128)(2,1)S(1)}, bf16[256,256]{1,0:T(8,128)(2,1)}, u32[]{:S(2)}) copy-start(bf16[256,256]{1,0:T(8,128)(2,1)} %preact.1) | copy-start | bytes 393220
  3.5 11.6 %copy-start.4 = (bf16[256,256]{1,0:T(8,128)(2,1)S(1)}, bf16[256,256]{1,0:T(8,128)(2,1)}, u32[]{:S(2)}) copy-start(bf16[256,256]{1,0:T(8,128)(2,1)} %w_neigh.1) | copy-start | bytes 393220
  3.5 11.6 %copy-start.5 = (bf16[256,256]{1,0:T(8,128)(2,1)S(1)}, bf16[256,256]{1,0:T(8,128)(2,1)}, u32[]{:S(2)}) copy-start(bf16[256,256]{1,0:T(8,128)(2,1)} %w_self.1) | copy-start | bytes 393220
  3.5 25.2 %all-to-all-start = ((bf16[8,192,128]{2,1,0:T(8,128)(2,1)}), bf16[8,192,128]{2,1,0:T(8,128)(2,1)S(1)}, u32[]{:S(2)}, u32[]{:S(2)}) async-start(bf16[8,192,128]{2,1,0:T(8,128)(2,1)} %shard_map.227), calls=%async_computation | async-start | bytes 786432 | tf_op jit(solution)/shard_map/all_to_all | solution.py:271
  14.5 0.9 %copy-start.1 = (bf16[256,256]{1,0:T(8,128)(2,1)S(1)}, bf16[256,256]{1,0:T(8,128)(2,1)}, u32[]{:S(2)}) copy-start(bf16[256,256]{1,0:T(8,128)(2,1)} %grad_out.1) | copy-start | bytes 393220
  14.8 0.8 copy-start.6
  14.8 0.8 copy-start.12
  15.0 0.7 copy-start.9
  15.0 0.7 copy-start.10
  15.0 0.7 copy-start.11
  15.7 13.0 %copy-start.3 = (bf16[256,256]{1,0:T(8,128)(2,1)S(1)}, bf16[256,256]{1,0:T(8,128)(2,1)}, u32[]{:S(2)}) copy-start(bf16[256,256]{1,0:T(8,128)(2,1)} %feats.1) | copy-start | bytes 393220
  17.4 11.3 %copy-start.8 = (s32[1,8,128]{2,1,0:T(8,128)S(1)}, s32[1,8,128]{2,1,0:T(8,128)}, u32[]{:S(2)}) copy-start(s32[1,8,128]{2,1,0:T(8,128)} %param.39) | copy-start | bytes 12292
  55.2 5.0 %copy-start.7 = (bf16[256,64]{0,1:T(8,128)(2,1)S(1)}, bf16[256,64]{0,1:T(8,128)(2,1)}, u32[]{:S(2)}) copy-start(bf16[256,64]{0,1:T(8,128)(2,1)} %param.27) | copy-start | bytes 98308
  55.2 16.3 %all-to-all-start.2 = ((bf16[192,2,128]{2,1,0:T(2,128)(2,1)}), bf16[192,2,128]{2,1,0:T(2,128)(2,1)S(1)}, u32[]{:S(2)}, u32[]{:S(2)}) async-start(bf16[192,2,128]{2,1,0:T(2,128)(2,1)} %bitcast.5), calls=%async_computation.2 | async-start | bytes 196608 | tf_op jit(solution)/shard_map/all_to_all | solution.py:313

commit v5 on v4

--- a/solution.py
+++ b/solution.py
@@ -50,15 +50,16 @@
 
 
 def first_kernel(
-    xrow_in, xcol_in, xid_in, xcount_in, grad_in, preact_in, lift_in, tiles_in, feats_in, agg_in,
+    xrow_in, xcol_in, xid_in, xcount_in, grad_in, preact_in, lift_in, tiles_in, feats_in, agg_in, coords_in,
     s1_out,
-    xrow, xcol, xid, xcount, grad, preact, lift, tiles, feats, agg, cg, acc, sems,
+    xrow, xcol, xid, xcount, grad, preact, lift, tiles, feats, agg, coords, cg, acc, sems,
 ):
     groups = acc.shape[0]
     rank = acc.shape[1]
     pairs = (
         (grad_in, grad), (preact_in, preact), (lift_in, lift), (xrow_in, xrow), (xcol_in, xcol),
         (xid_in, xid), (xcount_in, xcount), (tiles_in, tiles), (feats_in, feats), (agg_in, agg),
+        (coords_in, coords),
     )
     copies = [
         pltpu.make_async_copy(source, target, sems.at[i])
@@ -81,6 +82,12 @@
             s1_out[j, at : at + step, :] = rows[:, :BLOCK]
             s1_out[j, at + step : at + 2 * step, :] = rows[:, BLOCK:]
         at += 2 * step
+    part = dot_nn(coords[...], gp)
+    step = rank // groups
+    for j in range(groups):
+        rows = part[j * step : (j + 1) * step]
+        halves = jnp.concatenate([rows[:, :BLOCK], rows[:, BLOCK:]], axis=0)
+        s1_out[j, at : at + 2 * step, :] = halves.astype(BF16)
     acc[...] = jnp.zeros_like(acc)
     for t in range(xrow.shape[1]):
         acc[xcol[0, t]] += dot_nn(cg[xrow[0, t]], tiles[xid[0, t]])
@@ -90,13 +97,12 @@
 
 
 def inner_kernel(
-    trow, tcol, tid, counts, grad_out, preact, cross, w_neigh, w_self, tiles,
-    base_out, bnd_out, lift_out, ng, acc,
+    trow, tcol, tid, counts, grad_out, preact, w_neigh, w_self, tiles,
+    base_out, bnd_out, ng, acc,
 ):
     cap = bnd_out.shape[1]
     blocks = ng.shape[0]
     gp = masked(grad_out, preact)
-    lift_out[...] = dot_nn(cross[...], gp)
     own = dot_nt(gp, w_self[...])
     grad = dot_nt(gp, w_neigh[...]).astype(BF16)
     for b in range(blocks):
@@ -114,13 +120,13 @@
         bnd_out[q] = jnp.where(slot < counts[0, q], rows, 0.0)
 
 
-def second_kernel(s1, xrecv, feats, lift_part, bnd, coords_out, s2_out, scr):
+def second_kernel(s1, xrecv, feats, bnd, coords_out, s2_out, scr):
     groups = s1.shape[0]
-    rank = lift_part.shape[0]
+    rank = coords_out.shape[1]
     peers = bnd.shape[0]
     cap = bnd.shape[1]
     nodes = feats.shape[0]
-    wide = 2 * cap + 6
+    wide = 2 * cap + 10
     row = lax.broadcasted_iota(jnp.int32, (nodes, BLOCK), 0)
     total = None
     for g in range(groups):
@@ -136,11 +142,16 @@
     for q in range(peers):
         scr[q * wide : q * wide + cap, :] = bnd[q, :, :BLOCK]
         scr[q * wide + cap : q * wide + 2 * cap, :] = bnd[q, :, BLOCK:]
-    pieces = [summed[:peers], summed[peers:]]
-    for value in (proj_t, lift_part[...]):
-        pieces += [value[:, :BLOCK], value[:, BLOCK:]]
+    share = peers // 2
+    pieces = [summed[at * share : (at + 1) * share] for at in range(4)]
+    for h in range(2):
+        for at in range(2):
+            pieces.append(proj_t[at * share : (at + 1) * share, h * BLOCK : (h + 1) * BLOCK])
+    lift_rows = summed[4 * share :]
+    pieces += [jnp.concatenate([lift_rows, lift_rows], axis=0), jnp.zeros((share, BLOCK), F32)]
     for at, piece in enumerate(pieces):
-        scr[pl.ds(2 * cap + at, peers, stride=wide), :] = piece
+        twice = [piece[8 * (i // 2) : 8 * (i // 2) + 8] for i in range(peers // 8)]
+        scr[pl.ds(2 * cap + at, peers, stride=wide), :] = jnp.concatenate(twice, axis=0)
     s2_out[...] = scr[...].astype(BF16)
 
 
@@ -149,12 +160,12 @@
     wide = s2.shape[0] // peers
     scr[...] = s2[...].astype(F32)
     sums = [
-        jnp.sum(scr[pl.ds(wide - 6 + at, peers, stride=wide), :], axis=0, keepdims=True)
-        for at in range(6)
-    ]
+        jnp.sum(scr[pl.ds(wide - 10 + at, peers, stride=wide), :], axis=0, keepdims=True)
+        for at in range(9)
+    ] + [jnp.zeros((1, BLOCK), F32)]
     share = jnp.concatenate(sums * 8, axis=0).astype(BF16)
-    for j in range(8):
-        s3_out[48 * j : 48 * (j + 1), :] = share
+    for j in range(4):
+        s3_out[80 * j : 80 * (j + 1), :] = share
 
 
 def feats_kernel(s2, recv, base, coords, proj_t, out):
@@ -169,33 +180,35 @@
 
 def fourth_kernel(s3, s4_out, scr):
     scr[...] = s3[...].astype(F32)
-    peers = s3.shape[0] // 6
+    peers = s3.shape[0] // 10
     side = peers // 8
-    pieces = [scr[pl.ds(at, peers, stride=6), :] for at in range(2)]
-    for at in range(2, 6):
-        total = scr[pl.ds(at, side, stride=6), :]
+    pieces = [scr[pl.ds(at, peers, stride=10), :] for at in range(4)]
+    for at in range(4, 8):
+        total = scr[pl.ds(at, side, stride=10), :]
         for g in range(1, 8):
-            total = total + scr[pl.ds(g * side * 6 + at, side, stride=6), :]
+            total = total + scr[pl.ds(g * side * 10 + at, side, stride=10), :]
         pieces.append(total)
+    pieces.append(scr[pl.ds(8, peers, stride=10), :])
     share = jnp.concatenate(pieces, axis=0).astype(BF16)
     for j in range(s4_out.shape[0]):
         s4_out[j] = share
 
 
 def last_kernel(norm_scale, s4, self_out, neigh_out, lift_out, proj_out, square, flat):
-    groups = 8
     for j in range(s4.shape[0]):
         value = s4[j].astype(F32) * norm_scale
-        first = 16 * (j // 2) + j % 2
-        for kind in range(2):
-            for g in range(groups):
-                at = 64 * kind + 8 * g
-                square[2 * kind + first // 32, pl.ds(32 * g + first % 32, 8, stride=2), :] = value[
-                    at : at + 8
-                ]
+        first = 8 * (j // 2) + j % 2
+        for kind in range(4):
+            for g in range(8):
+                at = 32 * kind + 4 * g
+                square[kind, pl.ds(32 * g + first, 4, stride=2), :] = value[at : at + 4]
         for part in range(4):
-            at = 128 + 8 * part
-            flat[part, pl.ds(first, 8, stride=2), :] = value[at : at + 8]
+            at = 128 + 4 * part
+            flat[part // 2, pl.ds(32 * (part % 2) + first, 4, stride=2), :] = value[at : at + 4]
+        if j < 4:
+            for g in range(8):
+                at = 144 + 4 * g
+                flat[2 + j // 2, pl.ds(8 * g + j % 2, 4, stride=2), :] = value[at : at + 4]
     for h in range(2):
         lanes = slice(h * BLOCK, (h + 1) * BLOCK)
         self_out[:, lanes] = square[h]
@@ -205,15 +218,14 @@
 
 
 def device_groups(inner):
-    sizes = (("z", 8), ("x", 4), ("y", 8), ("core", 2))
+    sizes = (("z", 8), ("x", 4), ("side", 2), ("y", 4), ("core", 2))
     lists = {}
-    for z in range(8):
-        for x in range(4):
-            for y in range(8):
-                for core in range(2):
-                    place = {"z": z, "x": x, "y": y, "core": core}
-                    key = tuple(place[name] for name, _ in sizes if name not in inner)
-                    lists.setdefault(key, []).append(((z * 4 + x) * 8 + y) * 2 + core)
+    for device in range(512):
+        place, rest = {}, device
+        for name, size in reversed(sizes):
+            place[name], rest = rest % size, rest // size
+        key = tuple(place[name] for name, _ in sizes if name not in inner)
+        lists.setdefault(key, []).append(device)
     return [lists[key] for key in sorted(lists)]
 
 
@@ -246,24 +258,24 @@
     cap = recv_rows.shape[-1]
     blocks = nodes // BLOCK
     norm_scale = 1.0 / math.sqrt(nodes * peers * groups)
-    wide = 2 * cap + 6
+    wide = 2 * cap + 10
     both = ("hst", "dev")
 
     first_args = (
         cross_rows, cross_cols, cross_ids, cross_counts, grad_out, preact, lift, tile_values,
-        feats, neigh_agg,
+        feats, neigh_agg, cross_coords.T,
     )
     (s1,) = call(
         first_kernel,
-        (shape((groups, rank + 4 * width // groups, BLOCK), BF16),),
-        [HBM] * 10,
+        (shape((groups, rank + 4 * width // groups + 2 * rank // groups, BLOCK), BF16),),
+        [HBM] * 11,
         first_args,
         [pltpu.SMEM(v.shape, v.dtype) for v in first_args[:4]]
         + [pltpu.VMEM(v.shape, v.dtype) for v in first_args[4:]]
         + [
             pltpu.VMEM((blocks, rank, BLOCK), BF16),
             pltpu.VMEM((groups, rank, BLOCK), F32),
-            pltpu.SemaphoreType.DMA((10,)),
+            pltpu.SemaphoreType.DMA((11,)),
         ],
         flops=100_000_000,
         limit=60,
@@ -278,15 +290,14 @@
     )
     recv, sweep_rows = lax.optimization_barrier((recv, tile_rows))
     columns = blocks + peers * cap // BLOCK
-    base, bnd, lift_part = call(
+    base, bnd = call(
         inner_kernel,
         (
             shape((nodes, width), F32),
             shape((peers, cap, width), F32),
-            shape((rank, width), F32),
         ),
-        [SMEM] * 4 + [VMEM] * 6,
-        (sweep_rows, tile_cols, tile_ids, send_counts, grad_out, preact, cross_coords.T,
+        [SMEM] * 4 + [VMEM] * 5,
+        (sweep_rows, tile_cols, tile_ids, send_counts, grad_out, preact,
          w_neigh, w_self, tile_values),
         [pltpu.VMEM((blocks, BLOCK, width), BF16), pltpu.VMEM((columns, BLOCK, width), F32)],
         flops=350_000_000,
@@ -294,8 +305,8 @@
     coords, s2 = call(
         second_kernel,
         (shape((nodes, rank), BF16), shape((peers * wide, BLOCK), BF16)),
-        [VMEM] * 5,
-        (s1, cross_recv_rows.reshape(groups, BLOCK), feats, lift_part, bnd),
+        [VMEM] * 4,
+        (s1, cross_recv_rows.reshape(groups, BLOCK), feats, bnd),
         [pltpu.VMEM((peers * wide, BLOCK), F32)],
         flops=50_000_000,
     )
@@ -304,16 +315,16 @@
     ).reshape(peers * wide, BLOCK)
     (s3,) = call(
         third_kernel,
-        (shape((64 * 6, BLOCK), BF16),),
+        (shape((32 * 10, BLOCK), BF16),),
         [VMEM],
         (s2,),
         [pltpu.VMEM((peers * wide, BLOCK), F32)],
         flops=10_000_000,
     )
     s3 = lax.all_to_all(
-        s3.reshape(64 * 3, 2, BLOCK), both, split_axis=0, concat_axis=0, tiled=True,
+        s3.reshape(32 * 5, 2, BLOCK), both, split_axis=0, concat_axis=0, tiled=True,
         axis_index_groups=device_groups(("z", "y")),
-    ).reshape(64 * 6, BLOCK)
+    ).reshape(32 * 10, BLOCK)
     (grad_feats,) = call(
         feats_kernel,
         (shape((nodes, width), BF16),),
@@ -321,13 +332,12 @@
         (s2, recv, base, coords, proj.T),
         flops=150_000_000,
     )
-    s3, grad_feats = lax.optimization_barrier((s3, grad_feats))
     (s4,) = call(
         fourth_kernel,
-        (shape((8, 160, BLOCK), BF16),),
+        (shape((8, 176, BLOCK), BF16),),
         [VMEM],
         (s3,),
-        [pltpu.VMEM((64 * 6, BLOCK), F32)],
+        [pltpu.VMEM((32 * 10, BLOCK), F32)],
     )
     s4 = lax.all_to_all(
         s4, both, split_axis=0, concat_axis=0, tiled=True,

time: 85.8 us -> 85 us (level)
  waiting for transfers between devices: 21.4 us -> 18.7 us
  blocking collectives: 38.4 us -> 40 us
    all_to_all x1, waiting for transfers between devices: 10.1 us -> 6.45 us  [body(): lax.all_to_all(s4, both, split_axis=0, concat_axis=0, tiled=True, axis_in...]
    all_to_all x1, blocking collectives: 25.4 us -> 26.5 us  [body(): lax.all_to_all(s2.reshape(peers * wide // 2, 2, BLOCK), 'dev', split_axis...]
    all_to_all x1, waiting for transfers between devices: 11.3 us -> 12.3 us  [body(): s1 = lax.all_to_all(s1, 'hst', split_axis=0, concat_axis=0, tiled=True)]
where the time goes in v5:
time: 85 us; the launch traced here: 84.5 us
  blocking collectives  40 us (47%)
  waiting for transfers between devices  18.7 us (22%)
  starting transfers between devices  15.9 us (19%)
  Pallas kernels  7.97 us (9%)
  local copies, waits for them, and re-layouts  1.09 us (1%)
    all_to_all x1, blocking collectives, body(): lax.all_to_all(s2.reshape(peers * wide // 2, 2, BLOCK), 'dev', split_axis...  26.5 us
    all_to_all x1, blocking collectives, body(): lax.all_to_all(s3.reshape(32 * 5, 2, BLOCK), both, split_axis=0, concat_a...  13.5 us
    all_to_all x1, waiting for transfers between devices, body(): s1 = lax.all_to_all(s1, 'hst', split_axis=0, concat_axis=0, tiled=True)  12.3 us
    all_to_all x1, starting transfers between devices, body(): s1 = lax.all_to_all(s1, 'hst', split_axis=0, concat_axis=0, tiled=True)  11 us
    pallas_call x7, Pallas kernels, call(): pl.pallas_call(kernel, out_shape=tuple(outs), in_specs=specs, out_specs=t...  7.97 us
    all_to_all x1, waiting for transfers between devices, body(): lax.all_to_all(s4, both, split_axis=0, concat_axis=0, tiled=True, axis_in...  6.45 us
    all_to_all x1, starting transfers between devices, body(): lax.all_to_all(s4, both, split_axis=0, concat_axis=0, tiled=True, axis_in...  4.92 us
  transfers between devices with their start and end apart: 2, of which 2 were waited for; matrix products, arithmetic and copies ran while one was open for 1% of the time, Pallas kernels for 3%

profile of v5, /device:TPU:1, one launch (start us, length us, event | category | flops | bytes accessed | tf_op | source)
XLA Modules:
  0.0 84.5 jit_solution(13564863564234001539)
XLA Ops:
  0.6 0.0 copy-start.12
  0.6 0.0 copy-start.1
  0.7 0.0 copy-start.2
  0.7 0.0 copy-start.4
  0.7 0.0 copy-start.5
  0.7 2.8 %shard_map.227 = bf16[8,208,128]{2,1,0:T(8,128)(2,1)} custom-call(s32[1,8]{1,0:T(1,128)} %xrow_in.1, s32[1,8]{1,0:T(1,128)} %xcol_in.1, s32[1,8]{1,0:T(1,128)} %xid_in.1, s32[1,8]{1,0:T(1,128)} %xcount_in.1, bf16[256,256]{1,0:T(8,128)(2,1)} %grad_out.1, bf16[256,256]{1,0:T(8,128)(2,1)} %preact.1, bf16[64,256]{1,0:T(8,128)(2,1)} %lift_in.1, ...), custom_call_target="tpu_custom_call" | custom-call | flops 100000000 | bytes 2064512 | tf_op jit(solution)/shard_map/pallas_call | solution.py:33
  3.5 0.0 copy-start
  3.5 11.0 %all-to-all-start = ((bf16[8,208,128]{2,1,0:T(8,128)(2,1)}), bf16[8,208,128]{2,1,0:T(8,128)(2,1)S(1)}, u32[]{:S(2)}, u32[]{:S(2)}) async-start(bf16[8,208,128]{2,1,0:T(8,128)(2,1)} %shard_map.227), calls=%async_computation | async-start | bytes 851968 | tf_op jit(solution)/shard_map/all_to_all | solution.py:283
  14.5 0.0 copy-done.12
  14.5 0.1 copy.29
  14.6 0.1 fusion
  14.7 0.1 stack_reshape.6
  14.8 0.1 stack_reshape.7
  14.9 0.0 copy-start.8
  15.0 0.0 copy-start.9
  15.0 0.0 copy-start.10
  15.0 0.0 copy-start.11
  15.0 0.0 copy-done.1
  15.0 0.0 copy-done.2
  15.0 0.0 copy-done.4
  15.1 0.0 copy-done.5
  15.1 0.0 copy-done
  15.1 0.5 copy-done.8
  15.6 0.0 copy-done.9
  15.6 0.0 copy-done.10
  15.6 0.0 copy-done.11
  15.7 0.0 copy-start.3
  15.7 0.0 copy-start.7
  15.7 1.6 %shard_map.228 = (f32[256,256]{1,0:T(8,128)S(1)}, f32[64,8,256]{2,1,0:T(8,128)S(1)}) custom-call(s32[1,32]{1,0:T(1,128)S(1)} %copy-done.8, s32[1,32]{1,0:T(1,128)S(1)} %copy-done.9, s32[1,32]{1,0:T(1,128)S(1)} %copy-done.10, s32[1,64]{1,0:T(1,128)S(1)} %copy-done.11, bf16[256,256]{1,0:T(8,128)(2,1)S(1)} %copy-done.1, bf16[256,256]{1,0:T(8,128)(2,1)S(1)} %copy-done.2, ...), custom_call_target="tpu_custom_call" | custom-call | flops 350000000 | bytes 2359936 | tf_op jit(solution)/shard_map/pallas_call | solution.py:33
  17.3 12.3 %all-to-all-done.s1 = bf16[8,208,128]{2,1,0:T(8,128)(2,1)S(1)} async-done(((bf16[8,208,128]{2,1,0:T(8,128)(2,1)}), bf16[8,208,128]{2,1,0:T(8,128)(2,1)S(1)}, u32[]{:S(2)}, u32[]{:S(2)}) %all-to-all-start) | async-done | bytes 426016 | tf_op jit(solution)/shard_map/all_to_all | solution.py:283
  29.6 0.0 copy-done.3
  29.6 0.0 copy-done.7
  29.6 0.5 shard_map.229
  30.1 26.5 %all_to_all.20 = bf16[832,2,128]{2,1,0:T(2,128)(2,1)S(1)} all-to-all(bf16[832,2,128]{2,1,0:T(2,128)(2,1)S(1)} %bitcast.11), channel_id=1, replica_groups=mesh['hst'=8,'dev'=64] {'dev'}, dimensions={0} | all-to-all | bytes 851968 | tf_op jit(solution)/shard_map/all_to_all | solution.py:313
  56.5 0.1 shard_map.231
  56.6 13.5 %all_to_all.21 = bf16[160,2,128]{2,1,0:T(2,128)(2,1)S(1)} all-to-all(bf16[160,2,128]{2,1,0:T(2,128)(2,1)S(1)} %bitcast.13), channel_id=1, replica_groups={{0,2,4,6,64,66,68,70,128,130,132,134,192,194,196,198,256,258,260,262,32..., dimensions={0} | all-to-all | bytes 163840 | tf_op jit(solution)/shard_map/all_to_all | solution.py:324
  70.1 0.8 shard_map.232
  70.9 0.0 copy-start.6
  70.9 4.9 %all-to-all-start.3 = ((bf16[8,176,128]{2,1,0:T(8,128)(2,1)}), bf16[8,176,128]{2,1,0:T(8,128)(2,1)S(1)}, u32[]{:S(2)}, u32[]{:S(2)}) async-start(bf16[8,176,128]{2,1,0:T(8,128)(2,1)} %shard_map.232), calls=%async_computation.3 | async-start | bytes 720896 | tf_op jit(solution)/shard_map/all_to_all | solution.py:342
  75.8 0.0 copy-done.6
  75.8 1.3 %shard_map.230 = bf16[256,256]{1,0:T(8,128)(2,1)} custom-call(bf16[1664,128]{1,0:T(8,128)(2,1)S(1)} %bitcast.10, s32[2,1664]{1,0:T(2,128)S(1)} %pad_add_fusion.recv, f32[256,256]{1,0:T(8,128)S(1)} %get-tuple-element.19.base, bf16[256,64]{1,0:T(8,128)(2,1)S(1)} %get-tuple-element.20.coords, bf16[64,256]{1,0:T(8,128)(2,1)S(1)} %bitcast.14), custom_call_target="tpu_custom_call" | custom-call | flops 150000000 | bytes 898048 | tf_op jit(solution)/shard_map/pallas_call | solution.py:33
  77.1 6.5 %all-to-all-done.3.refs_0_ = bf16[8,176,128]{2,1,0:T(8,128)(2,1)S(1)} async-done(((bf16[8,176,128]{2,1,0:T(8,128)(2,1)}), bf16[8,176,128]{2,1,0:T(8,128)(2,1)S(1)}, u32[]{:S(2)}, u32[]{:S(2)}) %all-to-all-start.3) | async-done | bytes 360480 | tf_op jit(solution)/shard_map/all_to_all | solution.py:342
  83.6 1.0 %shard_map.233 = (f32[256,256]{1,0:T(8,128)}, f32[256,256]{1,0:T(8,128)}, f32[64,256]{1,0:T(8,128)}, f32[64,256]{1,0:T(8,128)}) custom-call(bf16[8,176,128]{2,1,0:T(8,128)(2,1)S(1)} %all-to-all-done.3.refs_0_), custom_call_target="tpu_custom_call" | custom-call | bytes 1015808 | tf_op jit(solution)/shard_map/pallas_call | solution.py:33
  (1 shorter events, 0.0 us)
Async XLA Ops:
  0.6 13.9 %copy-start.12 = (s32[1,64,8]{1,2,0:T(8,128)S(1)}, s32[1,64,8]{1,2,0:T(8,128)}, u32[]{:S(2)}) copy-start(s32[1,64,8]{1,2,0:T(8,128)} %param.37) | copy-start | bytes 6148
  0.6 14.4 %copy-start.1 = (bf16[256,256]{1,0:T(8,128)(2,1)S(1)}, bf16[256,256]{1,0:T(8,128)(2,1)}, u32[]{:S(2)}) copy-start(bf16[256,256]{1,0:T(8,128)(2,1)} %grad_out.1) | copy-start | bytes 393220
  0.7 14.4 %copy-start.2 = (bf16[256,256]{1,0:T(8,128)(2,1)S(1)}, bf16[256,256]{1,0:T(8,128)(2,1)}, u32[]{:S(2)}) copy-start(bf16[256,256]{1,0:T(8,128)(2,1)} %preact.1) | copy-start | bytes 393220
  0.7 14.4 %copy-start.4 = (bf16[256,256]{1,0:T(8,128)(2,1)S(1)}, bf16[256,256]{1,0:T(8,128)(2,1)}, u32[]{:S(2)}) copy-start(bf16[256,256]{1,0:T(8,128)(2,1)} %w_neigh.1) | copy-start | bytes 393220
  0.7 14.4 %copy-start.5 = (bf16[256,256]{1,0:T(8,128)(2,1)S(1)}, bf16[256,256]{1,0:T(8,128)(2,1)}, u32[]{:S(2)}) copy-start(bf16[256,256]{1,0:T(8,128)(2,1)} %w_self.1) | copy-start | bytes 393220
  3.5 11.6 %copy-start = (bf16[32,128,128]{2,1,0:T(8,128)(2,1)S(1)}, bf16[32,128,128]{2,1,0:T(8,128)(2,1)}, u32[]{:S(2)}) copy-start(bf16[32,128,128]{2,1,0:T(8,128)(2,1)} %tiles.1) | copy-start | bytes 3145732
  3.5 26.1 %all-to-all-start = ((bf16[8,208,128]{2,1,0:T(8,128)(2,1)}), bf16[8,208,128]{2,1,0:T(8,128)(2,1)S(1)}, u32[]{:S(2)}, u32[]{:S(2)}) async-start(bf16[8,208,128]{2,1,0:T(8,128)(2,1)} %shard_map.227), calls=%async_computation | async-start | bytes 851968 | tf_op jit(solution)/shard_map/all_to_all | solution.py:283
  14.9 0.7 copy-start.8
  15.0 0.7 copy-start.9
  15.0 0.7 copy-start.10
  15.0 0.7 copy-start.11
  15.7 13.9 %copy-start.3 = (bf16[256,256]{1,0:T(8,128)(2,1)S(1)}, bf16[256,256]{1,0:T(8,128)(2,1)}, u32[]{:S(2)}) copy-start(bf16[256,256]{1,0:T(8,128)(2,1)} %feats.1) | copy-start | bytes 393220
  15.7 13.9 %copy-start.7 = (s32[1,8,128]{2,1,0:T(8,128)S(1)}, s32[1,8,128]{2,1,0:T(8,128)}, u32[]{:S(2)}) copy-start(s32[1,8,128]{2,1,0:T(8,128)} %param.39) | copy-start | bytes 12292
  70.9 4.9 %copy-start.6 = (bf16[256,64]{0,1:T(8,128)(2,1)S(1)}, bf16[256,64]{0,1:T(8,128)(2,1)}, u32[]{:S(2)}) copy-start(bf16[256,64]{0,1:T(8,128)(2,1)} %param.27) | copy-start | bytes 98308
  70.9 12.7 %all-to-all-start.3 = ((bf16[8,176,128]{2,1,0:T(8,128)(2,1)}), bf16[8,176,128]{2,1,0:T(8,128)(2,1)S(1)}, u32[]{:S(2)}, u32[]{:S(2)}) async-start(bf16[8,176,128]{2,1,0:T(8,128)(2,1)} %shard_map.232), calls=%async_computation.3 | async-start | bytes 720896 | tf_op jit(solution)/shard_map/all_to_all | solution.py:342

commit v6 on v5

--- a/solution.py
+++ b/solution.py
@@ -10,6 +10,7 @@
 F32 = jnp.float32
 BF16 = jnp.bfloat16
 BLOCK = 128
+ROOM = 32
 
 VMEM = pl.BlockSpec(memory_space=pltpu.VMEM)
 SMEM = pl.BlockSpec(memory_space=pltpu.SMEM)
@@ -152,13 +153,13 @@
     for at, piece in enumerate(pieces):
         twice = [piece[8 * (i // 2) : 8 * (i // 2) + 8] for i in range(peers // 8)]
         scr[pl.ds(2 * cap + at, peers, stride=wide), :] = jnp.concatenate(twice, axis=0)
-    s2_out[...] = scr[...].astype(BF16)
+    s2_out[...] = scr[: s2_out.shape[0]].astype(BF16)
 
 
 def third_kernel(s2, s3_out, scr):
     peers = 64
     wide = s2.shape[0] // peers
-    scr[...] = s2[...].astype(F32)
+    scr[: s2.shape[0], :] = s2[...].astype(F32)
     sums = [
         jnp.sum(scr[pl.ds(wide - 10 + at, peers, stride=wide), :], axis=0, keepdims=True)
         for at in range(9)
@@ -179,7 +180,7 @@
 
 
 def fourth_kernel(s3, s4_out, scr):
-    scr[...] = s3[...].astype(F32)
+    scr[: s3.shape[0], :] = s3[...].astype(F32)
     peers = s3.shape[0] // 10
     side = peers // 8
     pieces = [scr[pl.ds(at, peers, stride=10), :] for at in range(4)]
@@ -211,10 +212,10 @@
                 flat[2 + j // 2, pl.ds(8 * g + j % 2, 4, stride=2), :] = value[at : at + 4]
     for h in range(2):
         lanes = slice(h * BLOCK, (h + 1) * BLOCK)
-        self_out[:, lanes] = square[h]
-        neigh_out[:, lanes] = square[2 + h]
-        proj_out[:, lanes] = flat[h]
-        lift_out[:, lanes] = flat[2 + h]
+        self_out[:, lanes] = square[h, : self_out.shape[0]]
+        neigh_out[:, lanes] = square[2 + h, : neigh_out.shape[0]]
+        proj_out[:, lanes] = flat[h, : proj_out.shape[0]]
+        lift_out[:, lanes] = flat[2 + h, : lift_out.shape[0]]
 
 
 def device_groups(inner):
@@ -307,7 +308,7 @@
         (shape((nodes, rank), BF16), shape((peers * wide, BLOCK), BF16)),
         [VMEM] * 4,
         (s1, cross_recv_rows.reshape(groups, BLOCK), feats, bnd),
-        [pltpu.VMEM((peers * wide, BLOCK), F32)],
+        [pltpu.VMEM((peers * wide + ROOM, BLOCK), F32)],
         flops=50_000_000,
     )
     s2 = lax.all_to_all(
@@ -318,7 +319,7 @@
         (shape((32 * 10, BLOCK), BF16),),
         [VMEM],
         (s2,),
-        [pltpu.VMEM((peers * wide, BLOCK), F32)],
+        [pltpu.VMEM((peers * wide + ROOM, BLOCK), F32)],
         flops=10_000_000,
     )
     s3 = lax.all_to_all(
@@ -337,7 +338,7 @@
         (shape((8, 176, BLOCK), BF16),),
         [VMEM],
         (s3,),
-        [pltpu.VMEM((32 * 10, BLOCK), F32)],
+        [pltpu.VMEM((32 * 10 + 2 * ROOM, BLOCK), F32)],
     )
     s4 = lax.all_to_all(
         s4, both, split_axis=0, concat_axis=0, tiled=True,
@@ -353,7 +354,7 @@
         ),
         [VMEM],
         (s4,),
-        [pltpu.VMEM((4, width, BLOCK), F32), pltpu.VMEM((4, rank, BLOCK), F32)],
+        [pltpu.VMEM((4, width + ROOM, BLOCK), F32), pltpu.VMEM((4, rank + ROOM, BLOCK), F32)],
     )
     return (grad_feats, grad_self, grad_neigh, grad_lift, grad_proj.T)
 

time: 85 us -> 85 us (level)
  no operation moved by 1% of the time
where the time goes in v6:
time: 85 us; the launch traced here: 84.5 us
  blocking collectives  40 us (47%)
  waiting for transfers between devices  18.7 us (22%)
  starting transfers between devices  15.9 us (19%)
  Pallas kernels  7.97 us (9%)
  local copies, waits for them, and re-layouts  1.09 us (1%)
    all_to_all x1, blocking collectives, body(): lax.all_to_all(s2.reshape(peers * wide // 2, 2, BLOCK), 'dev', split_axis...  26.5 us
    all_to_all x1, blocking collectives, body(): lax.all_to_all(s3.reshape(32 * 5, 2, BLOCK), both, split_axis=0, concat_a...  13.5 us
    all_to_all x1, waiting for transfers between devices, body(): s1 = lax.all_to_all(s1, 'hst', split_axis=0, concat_axis=0, tiled=True)  12.3 us
    all_to_all x1, starting transfers between devices, body(): s1 = lax.all_to_all(s1, 'hst', split_axis=0, concat_axis=0, tiled=True)  11 us
    pallas_call x7, Pallas kernels, call(): pl.pallas_call(kernel, out_shape=tuple(outs), in_specs=specs, out_specs=t...  7.97 us
    all_to_all x1, waiting for transfers between devices, body(): lax.all_to_all(s4, both, split_axis=0, concat_axis=0, tiled=True, axis_in...  6.45 us
    all_to_all x1, starting transfers between devices, body(): lax.all_to_all(s4, both, split_axis=0, concat_axis=0, tiled=True, axis_in...  4.92 us
  transfers between devices with their start and end apart: 2, of which 2 were waited for; matrix products, arithmetic and copies ran while one was open for 1% of the time, Pallas kernels for 3%

profile of v6, /device:TPU:1, one launch (start us, length us, event | category | flops | bytes accessed | tf_op | source)
XLA Modules:
  0.0 84.5 jit_solution(2019122742907981969)
XLA Ops:
  0.6 0.0 copy-start.12
  0.6 0.0 copy-start.1
  0.7 0.0 copy-start.2
  0.7 0.0 copy-start.4
  0.7 0.0 copy-start.5
  0.7 2.8 %shard_map.227 = bf16[8,208,128]{2,1,0:T(8,128)(2,1)} custom-call(s32[1,8]{1,0:T(1,128)} %xrow_in.1, s32[1,8]{1,0:T(1,128)} %xcol_in.1, s32[1,8]{1,0:T(1,128)} %xid_in.1, s32[1,8]{1,0:T(1,128)} %xcount_in.1, bf16[256,256]{1,0:T(8,128)(2,1)} %grad_out.1, bf16[256,256]{1,0:T(8,128)(2,1)} %preact.1, bf16[64,256]{1,0:T(8,128)(2,1)} %lift_in.1, ...), custom_call_target="tpu_custom_call" | custom-call | flops 100000000 | bytes 2064512 | tf_op jit(solution)/shard_map/pallas_call | solution.py:34
  3.5 0.0 copy-start
  3.5 11.0 %all-to-all-start = ((bf16[8,208,128]{2,1,0:T(8,128)(2,1)}), bf16[8,208,128]{2,1,0:T(8,128)(2,1)S(1)}, u32[]{:S(2)}, u32[]{:S(2)}) async-start(bf16[8,208,128]{2,1,0:T(8,128)(2,1)} %shard_map.227), calls=%async_computation | async-start | bytes 851968 | tf_op jit(solution)/shard_map/all_to_all | solution.py:284
  14.5 0.0 copy-done.12
  14.5 0.1 copy.29
  14.6 0.1 fusion
  14.7 0.1 stack_reshape.6
  14.8 0.1 stack_reshape.7
  14.9 0.0 copy-start.8
  15.0 0.0 copy-start.9
  15.0 0.0 copy-start.10
  15.0 0.0 copy-start.11
  15.0 0.0 copy-done.1
  15.0 0.0 copy-done.2
  15.0 0.0 copy-done.4
  15.1 0.0 copy-done.5
  15.1 0.0 copy-done
  15.1 0.5 copy-done.8
  15.6 0.0 copy-done.9
  15.6 0.0 copy-done.10
  15.6 0.0 copy-done.11
  15.7 0.0 copy-start.3
  15.7 0.0 copy-start.7
  15.7 1.6 %shard_map.228 = (f32[256,256]{1,0:T(8,128)S(1)}, f32[64,8,256]{2,1,0:T(8,128)S(1)}) custom-call(s32[1,32]{1,0:T(1,128)S(1)} %copy-done.8, s32[1,32]{1,0:T(1,128)S(1)} %copy-done.9, s32[1,32]{1,0:T(1,128)S(1)} %copy-done.10, s32[1,64]{1,0:T(1,128)S(1)} %copy-done.11, bf16[256,256]{1,0:T(8,128)(2,1)S(1)} %copy-done.1, bf16[256,256]{1,0:T(8,128)(2,1)S(1)} %copy-done.2, ...), custom_call_target="tpu_custom_call" | custom-call | flops 350000000 | bytes 2359936 | tf_op jit(solution)/shard_map/pallas_call | solution.py:34
  17.3 12.3 %all-to-all-done.s1 = bf16[8,208,128]{2,1,0:T(8,128)(2,1)S(1)} async-done(((bf16[8,208,128]{2,1,0:T(8,128)(2,1)}), bf16[8,208,128]{2,1,0:T(8,128)(2,1)S(1)}, u32[]{:S(2)}, u32[]{:S(2)}) %all-to-all-start) | async-done | bytes 426016 | tf_op jit(solution)/shard_map/all_to_all | solution.py:284
  29.6 0.0 copy-done.3
  29.6 0.0 copy-done.7
  29.6 0.5 shard_map.229
  30.1 26.5 %all_to_all.20 = bf16[832,2,128]{2,1,0:T(2,128)(2,1)S(1)} all-to-all(bf16[832,2,128]{2,1,0:T(2,128)(2,1)S(1)} %bitcast.11), channel_id=1, replica_groups=mesh['hst'=8,'dev'=64] {'dev'}, dimensions={0} | all-to-all | bytes 851968 | tf_op jit(solution)/shard_map/all_to_all | solution.py:314
  56.5 0.1 shard_map.231
  56.6 13.5 %all_to_all.21 = bf16[160,2,128]{2,1,0:T(2,128)(2,1)S(1)} all-to-all(bf16[160,2,128]{2,1,0:T(2,128)(2,1)S(1)} %bitcast.13), channel_id=1, replica_groups={{0,2,4,6,64,66,68,70,128,130,132,134,192,194,196,198,256,258,260,262,32..., dimensions={0} | all-to-all | bytes 163840 | tf_op jit(solution)/shard_map/all_to_all | solution.py:325
  70.1 0.8 shard_map.232
  70.9 0.0 copy-start.6
  70.9 4.9 %all-to-all-start.3 = ((bf16[8,176,128]{2,1,0:T(8,128)(2,1)}), bf16[8,176,128]{2,1,0:T(8,128)(2,1)S(1)}, u32[]{:S(2)}, u32[]{:S(2)}) async-start(bf16[8,176,128]{2,1,0:T(8,128)(2,1)} %shard_map.232), calls=%async_computation.3 | async-start | bytes 720896 | tf_op jit(solution)/shard_map/all_to_all | solution.py:343
  75.8 0.0 copy-done.6
  75.8 1.3 %shard_map.230 = bf16[256,256]{1,0:T(8,128)(2,1)} custom-call(bf16[1664,128]{1,0:T(8,128)(2,1)S(1)} %bitcast.10, s32[2,1664]{1,0:T(2,128)S(1)} %pad_add_fusion.recv, f32[256,256]{1,0:T(8,128)S(1)} %get-tuple-element.19.base, bf16[256,64]{1,0:T(8,128)(2,1)S(1)} %get-tuple-element.20.coords, bf16[64,256]{1,0:T(8,128)(2,1)S(1)} %bitcast.14), custom_call_target="tpu_custom_call" | custom-call | flops 150000000 | bytes 898048 | tf_op jit(solution)/shard_map/pallas_call | solution.py:34
  77.1 6.5 %all-to-all-done.3.refs_0_ = bf16[8,176,128]{2,1,0:T(8,128)(2,1)S(1)} async-done(((bf16[8,176,128]{2,1,0:T(8,128)(2,1)}), bf16[8,176,128]{2,1,0:T(8,128)(2,1)S(1)}, u32[]{:S(2)}, u32[]{:S(2)}) %all-to-all-start.3) | async-done | bytes 360480 | tf_op jit(solution)/shard_map/all_to_all | solution.py:343
  83.6 1.0 %shard_map.233 = (f32[256,256]{1,0:T(8,128)}, f32[256,256]{1,0:T(8,128)}, f32[64,256]{1,0:T(8,128)}, f32[64,256]{1,0:T(8,128)}) custom-call(bf16[8,176,128]{2,1,0:T(8,128)(2,1)S(1)} %all-to-all-done.3.refs_0_), custom_call_target="tpu_custom_call" | custom-call | bytes 1015808 | tf_op jit(solution)/shard_map/pallas_call | solution.py:34
  (1 shorter events, 0.0 us)
Async XLA Ops:
  0.6 13.9 %copy-start.12 = (s32[1,64,8]{1,2,0:T(8,128)S(1)}, s32[1,64,8]{1,2,0:T(8,128)}, u32[]{:S(2)}) copy-start(s32[1,64,8]{1,2,0:T(8,128)} %param.37) | copy-start | bytes 6148
  0.6 14.4 %copy-start.1 = (bf16[256,256]{1,0:T(8,128)(2,1)S(1)}, bf16[256,256]{1,0:T(8,128)(2,1)}, u32[]{:S(2)}) copy-start(bf16[256,256]{1,0:T(8,128)(2,1)} %grad_out.1) | copy-start | bytes 393220
  0.7 14.4 %copy-start.2 = (bf16[256,256]{1,0:T(8,128)(2,1)S(1)}, bf16[256,256]{1,0:T(8,128)(2,1)}, u32[]{:S(2)}) copy-start(bf16[256,256]{1,0:T(8,128)(2,1)} %preact.1) | copy-start | bytes 393220
  0.7 14.4 %copy-start.4 = (bf16[256,256]{1,0:T(8,128)(2,1)S(1)}, bf16[256,256]{1,0:T(8,128)(2,1)}, u32[]{:S(2)}) copy-start(bf16[256,256]{1,0:T(8,128)(2,1)} %w_neigh.1) | copy-start | bytes 393220
  0.7 14.4 %copy-start.5 = (bf16[256,256]{1,0:T(8,128)(2,1)S(1)}, bf16[256,256]{1,0:T(8,128)(2,1)}, u32[]{:S(2)}) copy-start(bf16[256,256]{1,0:T(8,128)(2,1)} %w_self.1) | copy-start | bytes 393220
  3.5 11.6 %copy-start = (bf16[32,128,128]{2,1,0:T(8,128)(2,1)S(1)}, bf16[32,128,128]{2,1,0:T(8,128)(2,1)}, u32[]{:S(2)}) copy-start(bf16[32,128,128]{2,1,0:T(8,128)(2,1)} %tiles.1) | copy-start | bytes 3145732
  3.5 26.1 %all-to-all-start = ((bf16[8,208,128]{2,1,0:T(8,128)(2,1)}), bf16[8,208,128]{2,1,0:T(8,128)(2,1)S(1)}, u32[]{:S(2)}, u32[]{:S(2)}) async-start(bf16[8,208,128]{2,1,0:T(8,128)(2,1)} %shard_map.227), calls=%async_computation | async-start | bytes 851968 | tf_op jit(solution)/shard_map/all_to_all | solution.py:284
  14.9 0.7 copy-start.8
  15.0 0.7 copy-start.9
  15.0 0.7 copy-start.10
  15.0 0.7 copy-start.11
  15.7 13.9 %copy-start.3 = (bf16[256,256]{1,0:T(8,128)(2,1)S(1)}, bf16[256,256]{1,0:T(8,128)(2,1)}, u32[]{:S(2)}) copy-start(bf16[256,256]{1,0:T(8,128)(2,1)} %feats.1) | copy-start | bytes 393220
  15.7 13.9 %copy-start.7 = (s32[1,8,128]{2,1,0:T(8,128)S(1)}, s32[1,8,128]{2,1,0:T(8,128)}, u32[]{:S(2)}) copy-start(s32[1,8,128]{2,1,0:T(8,128)} %param.39) | copy-start | bytes 12292
  70.9 4.9 %copy-start.6 = (bf16[256,64]{0,1:T(8,128)(2,1)S(1)}, bf16[256,64]{0,1:T(8,128)(2,1)}, u32[]{:S(2)}) copy-start(bf16[256,64]{0,1:T(8,128)(2,1)} %param.27) | copy-start | bytes 98308
  70.9 12.7 %all-to-all-start.3 = ((bf16[8,176,128]{2,1,0:T(8,128)(2,1)}), bf16[8,176,128]{2,1,0:T(8,128)(2,1)S(1)}, u32[]{:S(2)}, u32[]{:S(2)}) async-start(bf16[8,176,128]{2,1,0:T(8,128)(2,1)} %shard_map.232), calls=%async_computation.3 | async-start | bytes 720896 | tf_op jit(solution)/shard_map/all_to_all | solution.py:343

commit v7 on v6

--- a/solution.py
+++ b/solution.py
@@ -149,7 +149,10 @@
         for at in range(2):
             pieces.append(proj_t[at * share : (at + 1) * share, h * BLOCK : (h + 1) * BLOCK])
     lift_rows = summed[4 * share :]
-    pieces += [jnp.concatenate([lift_rows, lift_rows], axis=0), jnp.zeros((share, BLOCK), F32)]
+    side = BLOCK // 2
+    lift_rows = jnp.concatenate([lift_rows[:, :side], lift_rows[:, side:]], axis=0)
+    lift_rows = jnp.concatenate([lift_rows, jnp.zeros((share, side), F32)], axis=1)
+    pieces += [lift_rows, jnp.zeros((share, BLOCK), F32)]
     for at, piece in enumerate(pieces):
         twice = [piece[8 * (i // 2) : 8 * (i // 2) + 8] for i in range(peers // 8)]
         scr[pl.ds(2 * cap + at, peers, stride=wide), :] = jnp.concatenate(twice, axis=0)
@@ -189,15 +192,20 @@
         for g in range(1, 8):
             total = total + scr[pl.ds(g * side * 10 + at, side, stride=10), :]
         pieces.append(total)
-    pieces.append(scr[pl.ds(8, peers, stride=10), :])
+    lift = scr[pl.ds(8, peers, stride=10), :]
+    pieces.append(
+        jnp.concatenate(
+            [lift[: peers // 2, : BLOCK // 2], lift[peers // 2 :, : BLOCK // 2]], axis=1
+        )
+    )
     share = jnp.concatenate(pieces, axis=0).astype(BF16)
     for j in range(s4_out.shape[0]):
         s4_out[j] = share
 
 
 def last_kernel(norm_scale, s4, self_out, neigh_out, lift_out, proj_out, square, flat):
-    for j in range(s4.shape[0]):
-        value = s4[j].astype(F32) * norm_scale
+    values = [s4[j].astype(F32) * norm_scale for j in range(s4.shape[0])]
+    for j, value in enumerate(values):
         first = 8 * (j // 2) + j % 2
         for kind in range(4):
             for g in range(8):
@@ -207,9 +215,12 @@
             at = 128 + 4 * part
             flat[part // 2, pl.ds(32 * (part % 2) + first, 4, stride=2), :] = value[at : at + 4]
         if j < 4:
-            for g in range(8):
-                at = 144 + 4 * g
-                flat[2 + j // 2, pl.ds(8 * g + j % 2, 4, stride=2), :] = value[at : at + 4]
+            for part in range(2):
+                lanes = slice(part * BLOCK // 2, (part + 1) * BLOCK // 2)
+                lift = jnp.concatenate([value[144:, lanes], values[j + 4][144:, lanes]], axis=1)
+                for g in range(4):
+                    at = 8 * (4 * part + g) + j % 2
+                    flat[2 + j // 2, pl.ds(at, 4, stride=2), :] = lift[4 * g : 4 * g + 4]
     for h in range(2):
         lanes = slice(h * BLOCK, (h + 1) * BLOCK)
         self_out[:, lanes] = square[h, : self_out.shape[0]]
@@ -335,7 +346,7 @@
     )
     (s4,) = call(
         fourth_kernel,
-        (shape((8, 176, BLOCK), BF16),),
+        (shape((8, 160, BLOCK), BF16),),
         [VMEM],
         (s3,),
         [pltpu.VMEM((32 * 10 + 2 * ROOM, BLOCK), F32)],

time: 85 us -> 84.4 us (level)
  no operation moved by 1% of the time
where the time goes in v7:
time: 84.4 us; the launch traced here: 83.9 us
  blocking collectives  40 us (47%)
  waiting for transfers between devices  18.1 us (21%)
  starting transfers between devices  15.9 us (19%)
  Pallas kernels  7.97 us (9%)
  local copies, waits for them, and re-layouts  1.09 us (1%)
    all_to_all x1, blocking collectives, body(): lax.all_to_all(s2.reshape(peers * wide // 2, 2, BLOCK), 'dev', split_axis...  26.5 us
    all_to_all x1, blocking collectives, body(): lax.all_to_all(s3.reshape(32 * 5, 2, BLOCK), both, split_axis=0, concat_a...  13.5 us
    all_to_all x1, waiting for transfers between devices, body(): s1 = lax.all_to_all(s1, 'hst', split_axis=0, concat_axis=0, tiled=True)  12.3 us
    all_to_all x1, starting transfers between devices, body(): s1 = lax.all_to_all(s1, 'hst', split_axis=0, concat_axis=0, tiled=True)  11 us
    pallas_call x7, Pallas kernels, call(): pl.pallas_call(kernel, out_shape=tuple(outs), in_specs=specs, out_specs=t...  7.97 us
    all_to_all x1, waiting for transfers between devices, body(): lax.all_to_all(s4, both, split_axis=0, concat_axis=0, tiled=True, axis_in...  5.84 us
    all_to_all x1, starting transfers between devices, body(): lax.all_to_all(s4, both, split_axis=0, concat_axis=0, tiled=True, axis_in...  4.92 us
  transfers between devices with their start and end apart: 2, of which 2 were waited for; matrix products, arithmetic and copies ran while one was open for 1% of the time, Pallas kernels for 3%

profile of v7, /device:TPU:1, one launch (start us, length us, event | category | flops | bytes accessed | tf_op | source)
XLA Modules:
  0.0 83.9 jit_solution(8987231504899561206)
XLA Ops:
  0.6 0.0 copy-start.12
  0.6 0.0 copy-start.1
  0.7 0.0 copy-start.2
  0.7 0.0 copy-start.4
  0.7 0.0 copy-start.5
  0.7 2.8 %shard_map.227 = bf16[8,208,128]{2,1,0:T(8,128)(2,1)} custom-call(s32[1,8]{1,0:T(1,128)} %xrow_in.1, s32[1,8]{1,0:T(1,128)} %xcol_in.1, s32[1,8]{1,0:T(1,128)} %xid_in.1, s32[1,8]{1,0:T(1,128)} %xcount_in.1, bf16[256,256]{1,0:T(8,128)(2,1)} %grad_out.1, bf16[256,256]{1,0:T(8,128)(2,1)} %preact.1, bf16[64,256]{1,0:T(8,128)(2,1)} %lift_in.1, ...), custom_call_target="tpu_custom_call" | custom-call | flops 100000000 | bytes 2064512 | tf_op jit(solution)/shard_map/pallas_call | solution.py:34
  3.5 0.0 copy-start
  3.5 11.0 %all-to-all-start = ((bf16[8,208,128]{2,1,0:T(8,128)(2,1)}), bf16[8,208,128]{2,1,0:T(8,128)(2,1)S(1)}, u32[]{:S(2)}, u32[]{:S(2)}) async-start(bf16[8,208,128]{2,1,0:T(8,128)(2,1)} %shard_map.227), calls=%async_computation | async-start | bytes 851968 | tf_op jit(solution)/shard_map/all_to_all | solution.py:295
  14.5 0.0 copy-done.12
  14.5 0.1 copy.29
  14.6 0.1 fusion
  14.7 0.1 stack_reshape.6
  14.8 0.1 stack_reshape.7
  14.9 0.0 copy-start.8
  15.0 0.0 copy-start.9
  15.0 0.0 copy-start.10
  15.0 0.0 copy-start.11
  15.0 0.0 copy-done.1
  15.0 0.0 copy-done.2
  15.0 0.0 copy-done.4
  15.1 0.0 copy-done.5
  15.1 0.0 copy-done
  15.1 0.5 copy-done.8
  15.6 0.0 copy-done.9
  15.6 0.0 copy-done.10
  15.6 0.0 copy-done.11
  15.7 0.0 copy-start.3
  15.7 0.0 copy-start.7
  15.7 1.6 %shard_map.228 = (f32[256,256]{1,0:T(8,128)S(1)}, f32[64,8,256]{2,1,0:T(8,128)S(1)}) custom-call(s32[1,32]{1,0:T(1,128)S(1)} %copy-done.8, s32[1,32]{1,0:T(1,128)S(1)} %copy-done.9, s32[1,32]{1,0:T(1,128)S(1)} %copy-done.10, s32[1,64]{1,0:T(1,128)S(1)} %copy-done.11, bf16[256,256]{1,0:T(8,128)(2,1)S(1)} %copy-done.1, bf16[256,256]{1,0:T(8,128)(2,1)S(1)} %copy-done.2, ...), custom_call_target="tpu_custom_call" | custom-call | flops 350000000 | bytes 2359936 | tf_op jit(solution)/shard_map/pallas_call | solution.py:34
  17.3 12.3 %all-to-all-done.s1 = bf16[8,208,128]{2,1,0:T(8,128)(2,1)S(1)} async-done(((bf16[8,208,128]{2,1,0:T(8,128)(2,1)}), bf16[8,208,128]{2,1,0:T(8,128)(2,1)S(1)}, u32[]{:S(2)}, u32[]{:S(2)}) %all-to-all-start) | async-done | bytes 426016 | tf_op jit(solution)/shard_map/all_to_all | solution.py:295
  29.6 0.0 copy-done.3
  29.6 0.0 copy-done.7
  29.6 0.5 shard_map.229
  30.1 26.5 %all_to_all.20 = bf16[832,2,128]{2,1,0:T(2,128)(2,1)S(1)} all-to-all(bf16[832,2,128]{2,1,0:T(2,128)(2,1)S(1)} %bitcast.11), channel_id=1, replica_groups=mesh['hst'=8,'dev'=64] {'dev'}, dimensions={0} | all-to-all | bytes 851968 | tf_op jit(solution)/shard_map/all_to_all | solution.py:325
  56.5 0.1 shard_map.231
  56.6 13.5 %all_to_all.21 = bf16[160,2,128]{2,1,0:T(2,128)(2,1)S(1)} all-to-all(bf16[160,2,128]{2,1,0:T(2,128)(2,1)S(1)} %bitcast.12), channel_id=1, replica_groups={{0,2,4,6,64,66,68,70,128,130,132,134,192,194,196,198,256,258,260,262,32..., dimensions={0} | all-to-all | bytes 163840 | tf_op jit(solution)/shard_map/all_to_all | solution.py:336
  70.1 0.8 shard_map.232
  71.0 0.0 copy-start.6
  71.0 4.9 %all-to-all-start.3 = ((bf16[8,160,128]{2,1,0:T(8,128)(2,1)}), bf16[8,160,128]{2,1,0:T(8,128)(2,1)S(1)}, u32[]{:S(2)}, u32[]{:S(2)}) async-start(bf16[8,160,128]{2,1,0:T(8,128)(2,1)} %shard_map.232), calls=%async_computation.3 | async-start | bytes 655360 | tf_op jit(solution)/shard_map/all_to_all | solution.py:354
  75.9 0.0 copy-done.6
  75.9 1.3 %shard_map.230 = bf16[256,256]{1,0:T(8,128)(2,1)} custom-call(bf16[1664,128]{1,0:T(8,128)(2,1)S(1)} %bitcast.10, s32[2,1664]{1,0:T(2,128)S(1)} %pad_add_fusion.recv, f32[256,256]{1,0:T(8,128)S(1)} %get-tuple-element.19.base, bf16[256,64]{1,0:T(8,128)(2,1)S(1)} %get-tuple-element.20.coords, bf16[64,256]{1,0:T(8,128)(2,1)S(1)} %bitcast.14), custom_call_target="tpu_custom_call" | custom-call | flops 150000000 | bytes 898048 | tf_op jit(solution)/shard_map/pallas_call | solution.py:34
  77.2 5.8 %all-to-all-done.3.refs_0_ = bf16[8,160,128]{2,1,0:T(8,128)(2,1)S(1)} async-done(((bf16[8,160,128]{2,1,0:T(8,128)(2,1)}), bf16[8,160,128]{2,1,0:T(8,128)(2,1)S(1)}, u32[]{:S(2)}, u32[]{:S(2)}) %all-to-all-start.3) | async-done | bytes 327712 | tf_op jit(solution)/shard_map/all_to_all | solution.py:354
  83.0 0.9 %shard_map.233 = (f32[256,256]{1,0:T(8,128)}, f32[256,256]{1,0:T(8,128)}, f32[64,256]{1,0:T(8,128)}, f32[64,256]{1,0:T(8,128)}) custom-call(bf16[8,160,128]{2,1,0:T(8,128)(2,1)S(1)} %all-to-all-done.3.refs_0_), custom_call_target="tpu_custom_call" | custom-call | bytes 983040 | tf_op jit(solution)/shard_map/pallas_call | solution.py:34
  (1 shorter events, 0.0 us)
Async XLA Ops:
  0.6 13.9 %copy-start.12 = (s32[1,64,8]{1,2,0:T(8,128)S(1)}, s32[1,64,8]{1,2,0:T(8,128)}, u32[]{:S(2)}) copy-start(s32[1,64,8]{1,2,0:T(8,128)} %param.37) | copy-start | bytes 6148
  0.6 14.4 %copy-start.1 = (bf16[256,256]{1,0:T(8,128)(2,1)S(1)}, bf16[256,256]{1,0:T(8,128)(2,1)}, u32[]{:S(2)}) copy-start(bf16[256,256]{1,0:T(8,128)(2,1)} %grad_out.1) | copy-start | bytes 393220
  0.7 14.4 %copy-start.2 = (bf16[256,256]{1,0:T(8,128)(2,1)S(1)}, bf16[256,256]{1,0:T(8,128)(2,1)}, u32[]{:S(2)}) copy-start(bf16[256,256]{1,0:T(8,128)(2,1)} %preact.1) | copy-start | bytes 393220
  0.7 14.4 %copy-start.4 = (bf16[256,256]{1,0:T(8,128)(2,1)S(1)}, bf16[256,256]{1,0:T(8,128)(2,1)}, u32[]{:S(2)}) copy-start(bf16[256,256]{1,0:T(8,128)(2,1)} %w_neigh.1) | copy-start | bytes 393220
  0.7 14.4 %copy-start.5 = (bf16[256,256]{1,0:T(8,128)(2,1)S(1)}, bf16[256,256]{1,0:T(8,128)(2,1)}, u32[]{:S(2)}) copy-start(bf16[256,256]{1,0:T(8,128)(2,1)} %w_self.1) | copy-start | bytes 393220
  3.5 11.6 %copy-start = (bf16[32,128,128]{2,1,0:T(8,128)(2,1)S(1)}, bf16[32,128,128]{2,1,0:T(8,128)(2,1)}, u32[]{:S(2)}) copy-start(bf16[32,128,128]{2,1,0:T(8,128)(2,1)} %tiles.1) | copy-start | bytes 3145732
  3.5 26.1 %all-to-all-start = ((bf16[8,208,128]{2,1,0:T(8,128)(2,1)}), bf16[8,208,128]{2,1,0:T(8,128)(2,1)S(1)}, u32[]{:S(2)}, u32[]{:S(2)}) async-start(bf16[8,208,128]{2,1,0:T(8,128)(2,1)} %shard_map.227), calls=%async_computation | async-start | bytes 851968 | tf_op jit(solution)/shard_map/all_to_all | solution.py:295
  14.9 0.7 copy-start.8
  15.0 0.7 copy-start.9
  15.0 0.7 copy-start.10
  15.0 0.7 copy-start.11
  15.7 13.9 %copy-start.3 = (bf16[256,256]{1,0:T(8,128)(2,1)S(1)}, bf16[256,256]{1,0:T(8,128)(2,1)}, u32[]{:S(2)}) copy-start(bf16[256,256]{1,0:T(8,128)(2,1)} %feats.1) | copy-start | bytes 393220
  15.7 13.9 %copy-start.7 = (s32[1,8,128]{2,1,0:T(8,128)S(1)}, s32[1,8,128]{2,1,0:T(8,128)}, u32[]{:S(2)}) copy-start(s32[1,8,128]{2,1,0:T(8,128)} %param.39) | copy-start | bytes 12292
  71.0 4.9 %copy-start.6 = (bf16[256,64]{0,1:T(8,128)(2,1)S(1)}, bf16[256,64]{0,1:T(8,128)(2,1)}, u32[]{:S(2)}) copy-start(bf16[256,64]{0,1:T(8,128)(2,1)} %param.27) | copy-start | bytes 98308
  71.0 12.0 %all-to-all-start.3 = ((bf16[8,160,128]{2,1,0:T(8,128)(2,1)}), bf16[8,160,128]{2,1,0:T(8,128)(2,1)S(1)}, u32[]{:S(2)}, u32[]{:S(2)}) async-start(bf16[8,160,128]{2,1,0:T(8,128)(2,1)} %shard_map.232), calls=%async_computation.3 | async-start | bytes 655360 | tf_op jit(solution)/shard_map/all_to_all | solution.py:354

commit v8 on v7

--- a/solution.py
+++ b/solution.py
@@ -29,7 +29,7 @@
     return lax.dot_general(a, b, (((0,), (0,)), ((), ())), preferred_element_type=F32)
 
 
-def call(kernel, outs, specs, args, scratch=(), flops=0, limit=40):
+def call(kernel, outs, specs, args, scratch=(), flops=0, limit=16):
     nbytes = sum(math.prod(o.shape) * o.dtype.itemsize for o in list(outs) + list(args))
     return pl.pallas_call(
         kernel,

time: 84.4 us -> 84.4 us (level)
  no operation moved by 1% of the time
where the time goes in v8:
time: 84.4 us; the launch traced here: 83.9 us
  blocking collectives  40 us (47%)
  waiting for transfers between devices  18.1 us (21%)
  starting transfers between devices  15.9 us (19%)
  Pallas kernels  7.98 us (9%)
  local copies, waits for them, and re-layouts  1.09 us (1%)
    all_to_all x1, blocking collectives, body(): lax.all_to_all(s2.reshape(peers * wide // 2, 2, BLOCK), 'dev', split_axis...  26.5 us
    all_to_all x1, blocking collectives, body(): lax.all_to_all(s3.reshape(32 * 5, 2, BLOCK), both, split_axis=0, concat_a...  13.5 us
    all_to_all x1, waiting for transfers between devices, body(): s1 = lax.all_to_all(s1, 'hst', split_axis=0, concat_axis=0, tiled=True)  12.3 us
    all_to_all x1, starting transfers between devices, body(): s1 = lax.all_to_all(s1, 'hst', split_axis=0, concat_axis=0, tiled=True)  11 us
    pallas_call x7, Pallas kernels, call(): pl.pallas_call(kernel, out_shape=tuple(outs), in_specs=specs, out_specs=t...  7.98 us
    all_to_all x1, waiting for transfers between devices, body(): lax.all_to_all(s4, both, split_axis=0, concat_axis=0, tiled=True, axis_in...  5.83 us
    all_to_all x1, starting transfers between devices, body(): lax.all_to_all(s4, both, split_axis=0, concat_axis=0, tiled=True, axis_in...  4.92 us
  transfers between devices with their start and end apart: 2, of which 2 were waited for; matrix products, arithmetic and copies ran while one was open for 1% of the time, Pallas kernels for 3%

profile of v8, /device:TPU:1, one launch (start us, length us, event | category | flops | bytes accessed | tf_op | source)
XLA Modules:
  0.0 83.9 jit_solution(16871171943631199423)
XLA Ops:
  0.6 0.0 copy-start.12
  0.6 0.0 copy-start.1
  0.7 0.0 copy-start.2
  0.7 0.0 copy-start.4
  0.7 0.0 copy-start.5
  0.7 2.8 %shard_map.227 = bf16[8,208,128]{2,1,0:T(8,128)(2,1)} custom-call(s32[1,8]{1,0:T(1,128)} %xrow_in.1, s32[1,8]{1,0:T(1,128)} %xcol_in.1, s32[1,8]{1,0:T(1,128)} %xid_in.1, s32[1,8]{1,0:T(1,128)} %xcount_in.1, bf16[256,256]{1,0:T(8,128)(2,1)} %grad_out.1, bf16[256,256]{1,0:T(8,128)(2,1)} %preact.1, bf16[64,256]{1,0:T(8,128)(2,1)} %lift_in.1, ...), custom_call_target="tpu_custom_call" | custom-call | flops 100000000 | bytes 2064512 | tf_op jit(solution)/shard_map/pallas_call | solution.py:34
  3.5 0.0 copy-start
  3.5 11.0 %all-to-all-start = ((bf16[8,208,128]{2,1,0:T(8,128)(2,1)}), bf16[8,208,128]{2,1,0:T(8,128)(2,1)S(1)}, u32[]{:S(2)}, u32[]{:S(2)}) async-start(bf16[8,208,128]{2,1,0:T(8,128)(2,1)} %shard_map.227), calls=%async_computation | async-start | bytes 851968 | tf_op jit(solution)/shard_map/all_to_all | solution.py:295
  14.5 0.0 copy-done.12
  14.5 0.1 copy.29
  14.6 0.1 fusion
  14.7 0.1 stack_reshape.6
  14.8 0.1 stack_reshape.7
  15.0 0.0 copy-start.8
  15.0 0.0 copy-start.9
  15.0 0.0 copy-start.10
  15.0 0.0 copy-start.11
  15.0 0.0 copy-done.1
  15.0 0.0 copy-done.2
  15.0 0.0 copy-done.4
  15.1 0.0 copy-done.5
  15.1 0.0 copy-done
  15.1 0.5 copy-done.8
  15.6 0.0 copy-done.9
  15.6 0.0 copy-done.10
  15.6 0.0 copy-done.11
  15.7 0.0 copy-start.3
  15.7 0.0 copy-start.7
  15.7 1.6 %shard_map.228 = (f32[256,256]{1,0:T(8,128)S(1)}, f32[64,8,256]{2,1,0:T(8,128)S(1)}) custom-call(s32[1,32]{1,0:T(1,128)S(1)} %copy-done.8, s32[1,32]{1,0:T(1,128)S(1)} %copy-done.9, s32[1,32]{1,0:T(1,128)S(1)} %copy-done.10, s32[1,64]{1,0:T(1,128)S(1)} %copy-done.11, bf16[256,256]{1,0:T(8,128)(2,1)S(1)} %copy-done.1, bf16[256,256]{1,0:T(8,128)(2,1)S(1)} %copy-done.2, ...), custom_call_target="tpu_custom_call" | custom-call | flops 350000000 | bytes 2359936 | tf_op jit(solution)/shard_map/pallas_call | solution.py:34
  17.3 12.3 %all-to-all-done.s1 = bf16[8,208,128]{2,1,0:T(8,128)(2,1)S(1)} async-done(((bf16[8,208,128]{2,1,0:T(8,128)(2,1)}), bf16[8,208,128]{2,1,0:T(8,128)(2,1)S(1)}, u32[]{:S(2)}, u32[]{:S(2)}) %all-to-all-start) | async-done | bytes 426016 | tf_op jit(solution)/shard_map/all_to_all | solution.py:295
  29.6 0.0 copy-done.3
  29.6 0.0 copy-done.7
  29.6 0.5 shard_map.229
  30.1 26.5 %all_to_all.20 = bf16[832,2,128]{2,1,0:T(2,128)(2,1)S(1)} all-to-all(bf16[832,2,128]{2,1,0:T(2,128)(2,1)S(1)} %bitcast.11), channel_id=1, replica_groups=mesh['hst'=8,'dev'=64] {'dev'}, dimensions={0} | all-to-all | bytes 851968 | tf_op jit(solution)/shard_map/all_to_all | solution.py:325
  56.5 0.1 shard_map.231
  56.6 13.5 %all_to_all.21 = bf16[160,2,128]{2,1,0:T(2,128)(2,1)S(1)} all-to-all(bf16[160,2,128]{2,1,0:T(2,128)(2,1)S(1)} %bitcast.12), channel_id=1, replica_groups={{0,2,4,6,64,66,68,70,128,130,132,134,192,194,196,198,256,258,260,262,32..., dimensions={0} | all-to-all | bytes 163840 | tf_op jit(solution)/shard_map/all_to_all | solution.py:336
  70.1 0.8 shard_map.232
  71.0 0.0 copy-start.6
  71.0 4.9 %all-to-all-start.3 = ((bf16[8,160,128]{2,1,0:T(8,128)(2,1)}), bf16[8,160,128]{2,1,0:T(8,128)(2,1)S(1)}, u32[]{:S(2)}, u32[]{:S(2)}) async-start(bf16[8,160,128]{2,1,0:T(8,128)(2,1)} %shard_map.232), calls=%async_computation.3 | async-start | bytes 655360 | tf_op jit(solution)/shard_map/all_to_all | solution.py:354
  75.9 0.0 copy-done.6
  75.9 1.3 %shard_map.230 = bf16[256,256]{1,0:T(8,128)(2,1)} custom-call(bf16[1664,128]{1,0:T(8,128)(2,1)S(1)} %bitcast.10, s32[2,1664]{1,0:T(2,128)S(1)} %pad_add_fusion.recv, f32[256,256]{1,0:T(8,128)S(1)} %get-tuple-element.19.base, bf16[256,64]{1,0:T(8,128)(2,1)S(1)} %get-tuple-element.20.coords, bf16[64,256]{1,0:T(8,128)(2,1)S(1)} %bitcast.14), custom_call_target="tpu_custom_call" | custom-call | flops 150000000 | bytes 898048 | tf_op jit(solution)/shard_map/pallas_call | solution.py:34
  77.2 5.8 %all-to-all-done.3.refs_0_ = bf16[8,160,128]{2,1,0:T(8,128)(2,1)S(1)} async-done(((bf16[8,160,128]{2,1,0:T(8,128)(2,1)}), bf16[8,160,128]{2,1,0:T(8,128)(2,1)S(1)}, u32[]{:S(2)}, u32[]{:S(2)}) %all-to-all-start.3) | async-done | bytes 327712 | tf_op jit(solution)/shard_map/all_to_all | solution.py:354
  83.0 0.9 %shard_map.233 = (f32[256,256]{1,0:T(8,128)}, f32[256,256]{1,0:T(8,128)}, f32[64,256]{1,0:T(8,128)}, f32[64,256]{1,0:T(8,128)}) custom-call(bf16[8,160,128]{2,1,0:T(8,128)(2,1)S(1)} %all-to-all-done.3.refs_0_), custom_call_target="tpu_custom_call" | custom-call | bytes 983040 | tf_op jit(solution)/shard_map/pallas_call | solution.py:34
  (1 shorter events, 0.0 us)
Async XLA Ops:
  0.6 13.9 %copy-start.12 = (s32[1,64,8]{1,2,0:T(8,128)S(1)}, s32[1,64,8]{1,2,0:T(8,128)}, u32[]{:S(2)}) copy-start(s32[1,64,8]{1,2,0:T(8,128)} %param.37) | copy-start | bytes 6148
  0.6 14.4 %copy-start.1 = (bf16[256,256]{1,0:T(8,128)(2,1)S(1)}, bf16[256,256]{1,0:T(8,128)(2,1)}, u32[]{:S(2)}) copy-start(bf16[256,256]{1,0:T(8,128)(2,1)} %grad_out.1) | copy-start | bytes 393220
  0.7 14.4 %copy-start.2 = (bf16[256,256]{1,0:T(8,128)(2,1)S(1)}, bf16[256,256]{1,0:T(8,128)(2,1)}, u32[]{:S(2)}) copy-start(bf16[256,256]{1,0:T(8,128)(2,1)} %preact.1) | copy-start | bytes 393220
  0.7 14.4 %copy-start.4 = (bf16[256,256]{1,0:T(8,128)(2,1)S(1)}, bf16[256,256]{1,0:T(8,128)(2,1)}, u32[]{:S(2)}) copy-start(bf16[256,256]{1,0:T(8,128)(2,1)} %w_neigh.1) | copy-start | bytes 393220
  0.7 14.4 %copy-start.5 = (bf16[256,256]{1,0:T(8,128)(2,1)S(1)}, bf16[256,256]{1,0:T(8,128)(2,1)}, u32[]{:S(2)}) copy-start(bf16[256,256]{1,0:T(8,128)(2,1)} %w_self.1) | copy-start | bytes 393220
  3.5 11.6 %copy-start = (bf16[32,128,128]{2,1,0:T(8,128)(2,1)S(1)}, bf16[32,128,128]{2,1,0:T(8,128)(2,1)}, u32[]{:S(2)}) copy-start(bf16[32,128,128]{2,1,0:T(8,128)(2,1)} %tiles.1) | copy-start | bytes 3145732
  3.5 26.1 %all-to-all-start = ((bf16[8,208,128]{2,1,0:T(8,128)(2,1)}), bf16[8,208,128]{2,1,0:T(8,128)(2,1)S(1)}, u32[]{:S(2)}, u32[]{:S(2)}) async-start(bf16[8,208,128]{2,1,0:T(8,128)(2,1)} %shard_map.227), calls=%async_computation | async-start | bytes 851968 | tf_op jit(solution)/shard_map/all_to_all | solution.py:295
  15.0 0.7 copy-start.8
  15.0 0.7 copy-start.9
  15.0 0.7 copy-start.10
  15.0 0.7 copy-start.11
  15.7 13.9 %copy-start.3 = (bf16[256,256]{1,0:T(8,128)(2,1)S(1)}, bf16[256,256]{1,0:T(8,128)(2,1)}, u32[]{:S(2)}) copy-start(bf16[256,256]{1,0:T(8,128)(2,1)} %feats.1) | copy-start | bytes 393220
  15.7 13.9 %copy-start.7 = (s32[1,8,128]{2,1,0:T(8,128)S(1)}, s32[1,8,128]{2,1,0:T(8,128)}, u32[]{:S(2)}) copy-start(s32[1,8,128]{2,1,0:T(8,128)} %param.39) | copy-start | bytes 12292
  71.0 4.9 %copy-start.6 = (bf16[256,64]{0,1:T(8,128)(2,1)S(1)}, bf16[256,64]{0,1:T(8,128)(2,1)}, u32[]{:S(2)}) copy-start(bf16[256,64]{0,1:T(8,128)(2,1)} %param.27) | copy-start | bytes 98308
  71.0 12.0 %all-to-all-start.3 = ((bf16[8,160,128]{2,1,0:T(8,128)(2,1)}), bf16[8,160,128]{2,1,0:T(8,128)(2,1)S(1)}, u32[]{:S(2)}, u32[]{:S(2)}) async-start(bf16[8,160,128]{2,1,0:T(8,128)(2,1)} %shard_map.232), calls=%async_computation.3 | async-start | bytes 655360 | tf_op jit(solution)/shard_map/all_to_all | solution.py:354
